TPU v7x, 32 devices: a whole 2x2x4 slice. The times are simulated.
32 devices in a mesh: slab: 2 (over x), cell: 8 (over z, y), dp: 2 (over core).
Axes of the slice: x: 2, y: 2, z: 4, core: 2. Of those that a mesh axis runs over, the one named last changes fastest.
Arguments:
- sens: float32 [2, 2048, 32768], P(None, ('slab', 'dp'), 'cell'), parts along dimension 1, may hold values from -0.03125 to 0.03125
- observed: float32 [2, 2048], P(None, ('slab', 'dp')), parts along dimension 1, may hold values from -6 to 6
- noise: float32 [2, 2048], P(None, ('slab', 'dp')), parts along dimension 1, may hold values from 0.5 to 2
- survey_ids: int32 [2, 2048], P(None, ('slab', 'dp')), parts along dimension 1, may hold values from 0 to 7
- data_perturb: float32 [2, 8, 2048], P(None, None, ('slab', 'dp')), parts along dimension 2, may hold values from -6 to 6
- prior: float32 [2, 16, 32, 1024], P(None, 'slab', 'cell'), parts along dimension 1, may hold values from -6 to 6
Outputs:
- models: float32 [2, 16, 32, 1024], P(None, 'slab', 'cell'), parts along dimension 1
There are 2 independent parts, one for each index of `slab`. A program takes and returns all parts, laid end to end along the dimension named above; each array names one. Nothing has to cross between parts.
All inputs are finite; a program needn't handle non-finite values.
Results may differ from a plain program's by a relative error of at most 0.0001.
Values sent between devices are 32-bit elements; how exact they have to be, the bound alone decides.
No kernel may reach another device: no remote copies, remote signals or barrier semaphores. Data moves between devices by JAX's collectives and lax.ppermute only.
A program may use at most 64 MiB of HBM per device.

v0:
```python
import functools

import jax
import jax.numpy as jnp
from jax import lax
from jax.experimental import pallas as pl
from jax.experimental.pallas import tpu as pltpu
from jax.sharding import PartitionSpec as P

NX = 32
NSURV = 8
ITERS = 4

nu_value = 4.0
step_size = 0.5
couple_weight = 0.02
prior_weight = 0.1

LANES = 128
MIB = 2**20
BF16 = jnp.bfloat16
F32 = jnp.float32
IN_VMEM = pl.BlockSpec(memory_space=pltpu.VMEM)
IN_HBM = pl.BlockSpec(memory_space=pltpu.HBM)


def dot(left, right, along=0):
    return lax.dot_general(
        left, right, (((1,), (along,)), ((), ())), preferred_element_type=F32
    )


def resident(values):
    return pltpu.with_memory_space_constraint(values, pltpu.VMEM)


def split_rows(values):
    high = values.astype(BF16).astype(F32)
    return jnp.concatenate([high, values - high], axis=0).astype(BF16)


def fold_rows(values):
    half = values.shape[0] // 2
    return values[:half] + values[half:]


def prepare_kernel(
    block,
    sens_ref,
    prior_ref,
    ids_ref,
    split_ref,
    turned_ref,
    part_ref,
    count_ref,
    edge_ref,
    *rest,
):
    surveys, stations, _ = sens_ref.shape
    _, model_count, layers, layer_cells = prior_ref.shape
    flat_refs = rest[:surveys]
    buffers, prior_buffer, ids_buffer, semaphores, small_semaphores = rest[surveys:]
    per_survey = stations // block
    total = surveys * per_survey
    slots = buffers.shape[0]

    def copy(step):
        start = pl.multiple_of((step % per_survey) * block, block)
        slot = step % slots
        return pltpu.make_async_copy(
            sens_ref.at[step // per_survey, pl.ds(start, block), :],
            buffers.at[slot],
            semaphores.at[slot],
        )

    prior_copy = pltpu.make_async_copy(prior_ref, prior_buffer, small_semaphores.at[0])
    ids_copy = pltpu.make_async_copy(ids_ref, ids_buffer, small_semaphores.at[1])
    ahead = min(slots - 1, total)
    prior_copy.start()
    ids_copy.start()
    for step in range(min(2, ahead)):
        copy(step).start()
    prior_copy.wait()
    for step in range(min(2, ahead), ahead):
        copy(step).start()
    upward = lax.axis_index("dp") == 0
    for survey in range(surveys):
        layer_rows = [prior_buffer[survey, :, at, :] for at in range(layers)]
        for at in range(layers):
            flat_refs[survey][:, at * layer_cells : (at + 1) * layer_cells] = layer_rows[at]
        edge_ref[survey] = jnp.where(upward, layer_rows[0], layer_rows[-1])
    ids_copy.wait()
    lane = lax.broadcasted_iota(jnp.int32, (model_count, LANES), 1)
    for survey in range(surveys):
        ids = jnp.broadcast_to(ids_buffer[survey : survey + 1], (model_count, stations))
        counts = jnp.zeros((model_count, LANES), F32)
        for label in range(NSURV):
            here = jnp.sum((ids == label).astype(F32), axis=1, keepdims=True)
            counts = jnp.where(lane == NSURV + label, here, counts)
        count_ref[survey] = counts
    for survey in range(surveys):
        rows = split_rows(flat_refs[survey][...])

        def step_fn(at, carry):
            step = survey * per_survey + at
            copy(step).wait()

            @pl.when(step + slots - 1 < total)
            def _():
                copy(step + slots - 1).start()

            place = pl.ds(pl.multiple_of(at * block, block), block)
            values = buffers[step % slots]
            high = values.astype(BF16)
            low = (values - high.astype(F32)).astype(BF16)
            split_ref[0, survey, place, :] = high
            split_ref[1, survey, place, :] = low
            turned = values.T
            high_t = turned.astype(BF16)
            turned_ref[0, survey, :, place] = high_t
            turned_ref[1, survey, :, place] = (turned - high_t.astype(F32)).astype(BF16)
            part_ref[survey, :, place] = fold_rows(dot(rows, high, 1) + dot(rows, low, 1))
            return carry

        lax.fori_loop(0, per_survey, step_fn, 0)


def prepare(sens, prior, ids):
    surveys, stations, cells = sens.shape
    _, model_count, _, layer_cells = prior.shape
    block = min(stations, LANES)
    slots = 5
    outs = pl.pallas_call(
        functools.partial(prepare_kernel, block),
        out_shape=[
            pltpu.VMEM((2, surveys, stations, cells), BF16),
            pltpu.VMEM((2, surveys, cells, stations), BF16),
            jax.ShapeDtypeStruct((surveys, model_count, stations), F32),
            jax.ShapeDtypeStruct((surveys, model_count, LANES), F32),
            jax.ShapeDtypeStruct((surveys, model_count, layer_cells), F32),
        ]
        + [jax.ShapeDtypeStruct((model_count, cells), F32)] * surveys,
        in_specs=[IN_HBM] * 3,
        out_specs=[IN_VMEM] * (5 + surveys),
        scratch_shapes=[
            pltpu.VMEM((slots, block, cells), F32),
            pltpu.VMEM(prior.shape, F32),
            pltpu.VMEM(ids.shape, jnp.int32),
            pltpu.SemaphoreType.DMA((slots,)),
            pltpu.SemaphoreType.DMA((2,)),
        ],
        compiler_params=pltpu.CompilerParams(vmem_limit_bytes=12 * MIB),
        name="prepare",
    )(*[pltpu.with_memory_space_constraint(x, pltpu.HBM) for x in (sens, prior, ids)])
    return *outs[:5], list(outs[5:])


def stepped(models, prior, own, other):
    return models - step_size * ((own + other) + prior_weight * (models - prior))


def forward_kernel(survey, *refs):
    models_ref, prior_ref, own_ref, other_ref, turned_ref = refs[:5]
    models = stepped(models_ref[...], prior_ref[...], own_ref[...], other_ref[...])
    rows = split_rows(models)
    part = fold_rows(dot(rows, turned_ref[0, survey]) + dot(rows, turned_ref[1, survey]))
    refs = refs[5:]
    if survey + 1 < turned_ref.shape[1]:
        next_ref, part_ref = refs
        next_ref[...] = models
        part_ref[...] = part
        return
    earlier_models = refs[:survey]
    earlier_parts = refs[survey : 2 * survey]
    next_ref, edge_ref, part_ref = refs[2 * survey :]
    next_ref[...] = models
    part_ref[survey] = part
    for at in range(survey):
        part_ref[at] = earlier_parts[at][...]
    cells = models.shape[1]
    layer_cells = edge_ref.shape[2]
    upward = lax.axis_index("dp") == 0
    for at, ref in enumerate((*earlier_models, next_ref)):
        edge_ref[at] = jnp.where(
            upward, ref[:, :layer_cells], ref[:, cells - layer_cells :]
        )


def forward(models, prior, owns, others, turned, layer_cells):
    surveys = len(models)
    model_count, _ = models[0].shape
    stations = turned.shape[3]
    moved = []
    parts = []
    for survey in range(surveys):
        out_shape = [jax.ShapeDtypeStruct(models[survey].shape, F32)]
        operands = [models[survey], prior[survey], owns[survey], others[survey], resident(turned)]
        if survey + 1 < surveys:
            out_shape += [jax.ShapeDtypeStruct((model_count, stations), F32)]
        else:
            operands += moved + parts
            out_shape += [
                jax.ShapeDtypeStruct((surveys, model_count, layer_cells), F32),
                jax.ShapeDtypeStruct((surveys, model_count, stations), F32),
            ]
        outs = pl.pallas_call(
            functools.partial(forward_kernel, survey),
            out_shape=out_shape,
            in_specs=[IN_VMEM] * len(operands),
            out_specs=[IN_VMEM] * len(out_shape),
            compiler_params=pltpu.CompilerParams(vmem_limit_bytes=4 * MIB),
            cost_estimate=product_cost(turned),
            name="forward",
        )(*operands)
        moved.append(outs[0])
        parts.append(outs[1])
    return moved, outs[1], outs[2]


def product_cost(split):
    cells = split.shape[2] * split.shape[3]
    return pl.CostEstimate(flops=512 * cells, bytes_accessed=4 * cells, transcendentals=0)


def cross_terms(field, above, keep_x, keep_y, keep_z, depth_only):
    cells = field[0].shape[1]
    first = []
    second = []
    for grads, here, deeper in zip((first, second), field, above):
        grads.append((pltpu.roll(here, cells - 1, 1) - here) * keep_x)
        grads.append((pltpu.roll(here, cells - NX, 1) - here) * keep_y)
        change = deeper - here
        grads.append(change if keep_z is None else change * keep_z)
    cross_x = first[1] * second[2] - first[2] * second[1]
    cross_y = first[2] * second[0] - first[0] * second[2]
    cross_z = first[0] * second[1] - first[1] * second[0]
    scaling = (2.0 * couple_weight) / (
        1.0 + cross_x * cross_x + cross_y * cross_y + cross_z * cross_z
    )
    depth = [
        scaling * (second[0] * cross_y - second[1] * cross_x),
        scaling * (cross_x * first[1] - cross_y * first[0]),
    ]
    if keep_z is not None:
        depth = [value * keep_z for value in depth]
    if depth_only:
        return depth, None
    grad_x = [
        scaling * (second[1] * cross_z - second[2] * cross_y) * keep_x,
        scaling * (cross_y * first[2] - cross_z * first[1]) * keep_x,
    ]
    grad_y = [
        scaling * (second[2] * cross_x - second[0] * cross_z) * keep_y,
        scaling * (cross_z * first[0] - cross_x * first[2]) * keep_y,
    ]
    level = [
        (pltpu.roll(along_x, 1, 1) - along_x) + (pltpu.roll(along_y, NX, 1) - along_y)
        for along_x, along_y in zip(grad_x, grad_y)
    ]
    return depth, level


def couple_kernel(layer_cells, *refs):
    models_refs, edge_ref, out_refs = refs[:2], refs[2], refs[3:]
    model_count, cells = models_refs[0].shape
    layers = cells // layer_cells
    middle = layers // 2
    place = lax.broadcasted_iota(jnp.int32, (model_count, layer_cells), 1)
    keep_x = (place % NX < NX - 1).astype(F32)
    keep_y = (place < layer_cells - NX).astype(F32)
    side = lax.axis_index("dp")
    index = lax.axis_index("cell")

    def layer(at):
        if 0 <= at < layers:
            return [
                ref[:, at * layer_cells : (at + 1) * layer_cells] for ref in models_refs
            ]
        return [edge_ref[survey] for survey in range(2)]

    def write(start, stop):
        sums = {}

        def add(at, values):
            if 0 <= at < layers:
                sums[at] = values if at not in sums else [a + b for a, b in zip(sums[at], values)]

        for at in range(start, stop):
            keep_z = None
            if at < 0:
                keep_z = jnp.where(index > 0, 1.0, 0.0).astype(F32)
            elif at == layers - 1:
                keep_z = jnp.where(index < lax.axis_size("cell") - 1, 1.0, 0.0).astype(F32)
            depth, level = cross_terms(layer(at), layer(at + 1), keep_x, keep_y, keep_z, at < 0)
            if level is not None:
                add(at, [value - below for value, below in zip(level, depth)])
            add(at + 1, depth)
        for at in range(layers):
            for survey in range(2):
                spot = slice(at * layer_cells, (at + 1) * layer_cells)
                if at in sums:
                    out_refs[survey][:, spot] = sums[at][survey]
                else:
                    out_refs[survey][:, spot] = jnp.zeros((model_count, layer_cells), F32)

    @pl.when(side == 0)
    def _():
        write(middle, layers)

    @pl.when(side != 0)
    def _():
        write(-1, middle)


def couple_share(models, edge, layer_cells):
    return pl.pallas_call(
        functools.partial(couple_kernel, layer_cells),
        out_shape=[jax.ShapeDtypeStruct(x.shape, F32) for x in models],
        in_specs=[IN_VMEM] * 3,
        out_specs=[IN_VMEM] * 2,
        compiler_params=pltpu.CompilerParams(vmem_limit_bytes=4 * MIB),
        name="couple",
    )(*models, edge)


def residual_kernel(
    here_ref, there_ref, observed_ref, noise_ref, perturb_ref, ids_ref, count_ref, resid_ref, sums_ref
):
    surveys, model_count, stations = here_ref.shape
    lane = lax.broadcasted_iota(jnp.int32, (model_count, LANES), 1)
    for survey in range(surveys):
        noise = noise_ref[survey : survey + 1]
        targets = observed_ref[survey : survey + 1] + noise * perturb_ref[survey]
        resid = ((here_ref[survey] + there_ref[survey]) - targets) / noise
        resid_ref[survey] = resid
        squares = resid * resid
        ids = jnp.broadcast_to(ids_ref[survey : survey + 1], (model_count, stations))
        sums = count_ref[survey]
        for label in range(NSURV):
            here = jnp.sum(jnp.where(ids == label, squares, 0.0), axis=1, keepdims=True)
            sums = jnp.where(lane == label, here, sums)
        sums_ref[survey] = sums


def residual(here, there, observed, noise, perturb, ids, counts):
    return pl.pallas_call(
        residual_kernel,
        out_shape=[
            jax.ShapeDtypeStruct(here.shape, F32),
            jax.ShapeDtypeStruct(counts.shape, F32),
        ],
        in_specs=[IN_VMEM] * 7,
        out_specs=[IN_VMEM] * 2,
        compiler_params=pltpu.CompilerParams(vmem_limit_bytes=4 * MIB),
        name="residual",
    )(here, there, observed, noise, perturb, ids, counts)


def backward_kernel(
    survey, resid_ref, own_ref, other_ref, noise_ref, ids_ref, couple_ref, split_ref, out_ref
):
    _, model_count, stations = resid_ref.shape
    sums = own_ref[survey] + other_ref[survey]
    counts = pltpu.roll(sums, LANES - NSURV, 1)
    spread = (sums + 1.0) / (counts + 1.0)
    ids = jnp.broadcast_to(ids_ref[survey : survey + 1], (model_count, stations))
    spread_rows = jnp.zeros((model_count, stations), F32)
    for label in range(NSURV):
        spread_rows = jnp.where(ids == label, spread[:, label : label + 1], spread_rows)
    resid = resid_ref[survey]
    factor = (nu_value + 1.0) * resid / (
        noise_ref[survey : survey + 1] * (nu_value * spread_rows + resid * resid)
    )
    rows = split_rows(factor)
    out_ref[...] = couple_ref[...] + fold_rows(
        dot(rows, split_ref[0, survey]) + dot(rows, split_ref[1, survey])
    )


def backward(survey, resid, own, other, noise, ids, couple, split):
    return pl.pallas_call(
        functools.partial(backward_kernel, survey),
        out_shape=jax.ShapeDtypeStruct(couple.shape, F32),
        in_specs=[IN_VMEM] * 7,
        out_specs=IN_VMEM,
        compiler_params=pltpu.CompilerParams(vmem_limit_bytes=4 * MIB),
        cost_estimate=product_cost(split),
        name="backward",
    )(resid, own, other, noise, ids, couple, resident(split))


def step_kernel(models_ref, prior_ref, own_ref, other_ref, next_ref):
    next_ref[...] = stepped(models_ref[...], prior_ref[...], own_ref[...], other_ref[...])


def finish_kernel(*refs):
    out_ref = refs[-1]
    surveys, _, layers, layer_cells = out_ref.shape
    for survey in range(surveys):
        ready = survey + 1 < surveys
        models = refs[survey][...] if ready else stepped(*[ref[...] for ref in refs[survey:-1]])
        for at in range(layers):
            out_ref[survey, :, at, :] = models[:, at * layer_cells : (at + 1) * layer_cells]


def finish(models, prior, owns, others, shape):
    operands = []
    for survey in range(shape[0]):
        mine = [models[survey], prior[survey], owns[survey], others[survey]]
        if survey + 1 < shape[0]:
            mine = [
                pl.pallas_call(
                    step_kernel,
                    out_shape=jax.ShapeDtypeStruct(models[survey].shape, F32),
                    in_specs=[IN_VMEM] * 4,
                    out_specs=IN_VMEM,
                    compiler_params=pltpu.CompilerParams(vmem_limit_bytes=4 * MIB),
                    name="step",
                )(*mine)
            ]
        operands += mine
    return pl.pallas_call(
        finish_kernel,
        out_shape=jax.ShapeDtypeStruct(shape, F32),
        in_specs=[IN_VMEM] * len(operands),
        out_specs=IN_VMEM,
        compiler_params=pltpu.CompilerParams(vmem_limit_bytes=4 * MIB),
        name="finish",
    )(*operands)


def from_pair(values):
    return lax.ppermute(values, "dp", [(0, 1), (1, 0)])


def exchange_edges(edge):
    devices = lax.axis_size("cell")
    pairs = [(2 * i, 2 * i - 2) for i in range(1, devices)]
    pairs += [(2 * i + 1, 2 * i + 3) for i in range(devices - 1)]
    return lax.ppermute(edge, ("cell", "dp"), pairs)


def fetch(values, by, devices):
    return lax.ppermute(values, "cell", [(i, i ^ by) for i in range(devices)])


def cell_pair(values):
    devices = lax.axis_size("cell")
    stride = devices
    while stride > 2:
        base = 4 if stride >= 8 else 2
        stride //= base
        total = values
        for count in range(1, base):
            total = total + fetch(values, count * stride, devices)
        values = total
    return values, fetch(values, 1, devices)


def body(sens, observed, noise, ids, data_perturb, prior):
    surveys, _, _, layer_cells = prior.shape
    split, turned, part, counts, edge, flat = prepare(sens, prior, ids)
    models = flat
    for iteration in range(ITERS):
        if iteration:
            models, edge, part = forward(models, flat, owns, others, turned, layer_cells)
        edge = exchange_edges(edge)
        here, there = cell_pair(part)
        couple = couple_share(models, edge, layer_cells)
        resid, own_sums = residual(here, there, observed, noise, data_perturb, ids, counts)
        other_sums = from_pair(own_sums)
        owns = []
        others = []
        for survey in range(surveys):
            own = backward(
                survey, resid, own_sums, other_sums, noise, ids, couple[survey], split
            )
            owns.append(own)
            others.append(from_pair(own))
    return finish(models, flat, owns, others, prior.shape)


def solution(mesh):
    return jax.shard_map(
        body,
        mesh=mesh,
        in_specs=(
            P(None, ("slab", "dp"), "cell"),
            P(None, ("slab", "dp")),
            P(None, ("slab", "dp")),
            P(None, ("slab", "dp")),
            P(None, None, ("slab", "dp")),
            P(None, "slab", "cell", None),
        ),
        out_specs=P(None, "slab", "cell", None),
        check_vma=False,
    )
```

profile of v0, /device:TPU:0, one launch (start us, length us, event | category | flops | bytes accessed | tf_op | source)
XLA Modules:
  0.0 84.0 jit_solution(3268455637800616181)
XLA Ops:
  0.0 8.3 %prepare.1 = (bf16[2,2,512,4096]{3,2,1,0:T(8,128)(2,1)S(1)}, bf16[2,2,4096,512]{3,2,1,0:T(8,128)(2,1)S(1)}, f32[2,8,512]{2,1,0:T(8,128)S(1)}, f32[2,8,128]{2,1,0...) custom-call(f32[2,512,4096]{2,1,0:T(8,128)} %sens_ref.1, ...), custom_call_target="tpu_custom_call" | custom-call | tf_op jit(solution)/shard_map/prepare/pallas_call | solution.py:133
  8.3 5.1 %collective-permute-start.2 = (f32[2,8,512]{2,1,0:T(8,128)S(1)}, f32[2,8,512]{2,1,0:T(8,128)S(1)}, u32[]{:S(2)}, u32[]{:S(2)}) collective-permute-start(f32[2,8,512]{2,1,0:T(8,128)S(1)} %get-tuple-element.44), channel_id=1, source_target_pairs={{0,12},{2,14},{4,8},{6,10},{8,4},{10,6},{12,0},{14,2},{1,13},{3,15... | collective-permute-start | bytes 98312 | tf_op jit(solution)/shard_map/ppermute | solution.py:444
  14.1 1.3 %collective-permute-start.5 = (f32[2,8,1024]{2,1,0:T(8,128)S(1)}, f32[2,8,1024]{2,1,0:T(8,128)S(1)}, u32[]{:S(2)}, u32[]{:S(2)}) collective-permute-start(f32[2,8,1024]{2,1,0:T(8,128)S(1)} %get-tuple-element.49), channel_id=1, source_target_pairs={{2,0},{4,2},{6,4},{8,6},{10,8},{12,10},{14,12},{1,3},{3,5},{5,7},{... | collective-permute-start | bytes 196616 | tf_op jit(solution)/shard_map/ppermute | solution.py:440
  15.4 2.9 %collective-permute-done.1 = f32[2,8,512]{2,1,0:T(8,128)S(1)} collective-permute-done((f32[2,8,512]{2,1,0:T(8,128)S(1)}, f32[2,8,512]{2,1,0:T(8,128)S(1)}, u32[]{:S(2)}, u32[]{:S(2)}) %collective-permute-start.1) | collective-permute-done | bytes 32800 | tf_op jit(solution)/shard_map/ppermute | solution.py:444
  18.3 1.6 %collective-permute-start.3 = (f32[2,8,512]{2,1,0:T(8,128)S(1)}, f32[2,8,512]{2,1,0:T(8,128)S(1)}, u32[]{:S(2)}, u32[]{:S(2)}) collective-permute-start(f32[2,8,512]{2,1,0:T(8,128)S(1)} %add_add_fusion.3.here_ref), channel_id=1, source_target_pairs={{0,2},{2,0},{4,6},{6,4},{8,10},{10,8},{12,14},{14,12},{1,3},{3,1},... | collective-permute-start | bytes 98312 | tf_op jit(solution)/shard_map/ppermute | solution.py:444
  19.9 2.4 %collective-permute-done.3.there_ref = f32[2,8,512]{2,1,0:T(8,128)S(1)} collective-permute-done((f32[2,8,512]{2,1,0:T(8,128)S(1)}, f32[2,8,512]{2,1,0:T(8,128)S(1)}, u32[]{:S(2)}, u32[]{:S(2)}) %collective-permute-start.3) | collective-permute-done | bytes 32800 | tf_op jit(solution)/shard_map/ppermute | solution.py:444
  23.6 1.3 %backward.8.refs_2_ = f32[8,4096]{1,0:T(8,128)S(1)} custom-call(f32[2,8,512]{2,1,0:T(8,128)S(1)} %get-tuple-element.46.resid_ref, f32[2,8,128]{2,1,0:T(8,128)S(1)} %get-tuple-element.47.own_ref, f32[2,8,128]{2,1,0:T(8,128)S(1)} %collective-permute-done.4.other_ref, f32[2,512]{1,0:T(2,128)S(1)} %copy-done.1, s32[2,512]{1,0:T(2,128)S(1)} %copy-done, ...), custom_call_target="tpu_custom_call" | custom-call | flops 1073741824 | bytes 8388608 | tf_op jit(solution)/shard_map/backward/pallas_call | solution.py:381
  25.1 1.3 %backward.9.refs_2_ = f32[8,4096]{1,0:T(8,128)S(1)} custom-call(f32[2,8,512]{2,1,0:T(8,128)S(1)} %get-tuple-element.46.resid_ref, f32[2,8,128]{2,1,0:T(8,128)S(1)} %get-tuple-element.47.own_ref, f32[2,8,128]{2,1,0:T(8,128)S(1)} %collective-permute-done.4.other_ref, f32[2,512]{1,0:T(2,128)S(1)} %copy-done.1, s32[2,512]{1,0:T(2,128)S(1)} %copy-done, ...), custom_call_target="tpu_custom_call" | custom-call | flops 1073741824 | bytes 8388608 | tf_op jit(solution)/shard_map/backward/pallas_call | solution.py:381
  29.2 2.5 %collective-permute-start.10 = (f32[2,8,512]{2,1,0:T(8,128)S(1)}, f32[2,8,512]{2,1,0:T(8,128)S(1)}, u32[]{:S(2)}, u32[]{:S(2)}) collective-permute-start(f32[2,8,512]{2,1,0:T(8,128)S(1)} %get-tuple-element.56), channel_id=1, source_target_pairs={{0,12},{2,14},{4,8},{6,10},{8,4},{10,6},{12,0},{14,2},{1,13},{3,15... | collective-permute-start | bytes 98312 | tf_op jit(solution)/shard_map/ppermute | solution.py:444
  31.7 1.9 %collective-permute-start.8 = (f32[2,8,512]{2,1,0:T(8,128)S(1)}, f32[2,8,512]{2,1,0:T(8,128)S(1)}, u32[]{:S(2)}, u32[]{:S(2)}) collective-permute-start(f32[2,8,512]{2,1,0:T(8,128)S(1)} %get-tuple-element.56), channel_id=1, source_target_pairs={{0,4},{2,6},{4,0},{6,2},{8,12},{10,14},{12,8},{14,10},{1,5},{3,7},... | collective-permute-start | bytes 98312 | tf_op jit(solution)/shard_map/ppermute | solution.py:444
  33.6 1.3 %collective-permute-start.13 = (f32[2,8,1024]{2,1,0:T(8,128)S(1)}, f32[2,8,1024]{2,1,0:T(8,128)S(1)}, u32[]{:S(2)}, u32[]{:S(2)}) collective-permute-start(f32[2,8,1024]{2,1,0:T(8,128)S(1)} %get-tuple-element.60), channel_id=1, source_target_pairs={{2,0},{4,2},{6,4},{8,6},{10,8},{12,10},{14,12},{1,3},{3,5},{5,7},{... | collective-permute-start | bytes 196616 | tf_op jit(solution)/shard_map/ppermute | solution.py:440
  35.3 1.2 %collective-permute-done.9 = f32[2,8,512]{2,1,0:T(8,128)S(1)} collective-permute-done((f32[2,8,512]{2,1,0:T(8,128)S(1)}, f32[2,8,512]{2,1,0:T(8,128)S(1)}, u32[]{:S(2)}, u32[]{:S(2)}) %collective-permute-start.9) | collective-permute-done | bytes 32800 | tf_op jit(solution)/shard_map/ppermute | solution.py:444
  36.5 1.5 %collective-permute-start.11 = (f32[2,8,512]{2,1,0:T(8,128)S(1)}, f32[2,8,512]{2,1,0:T(8,128)S(1)}, u32[]{:S(2)}, u32[]{:S(2)}) collective-permute-start(f32[2,8,512]{2,1,0:T(8,128)S(1)} %add_add_fusion.2.here_ref), channel_id=1, source_target_pairs={{0,2},{2,0},{4,6},{6,4},{8,10},{10,8},{12,14},{14,12},{1,3},{3,1},... | collective-permute-start | bytes 98312 | tf_op jit(solution)/shard_map/ppermute | solution.py:444
  38.0 2.5 %collective-permute-done.11.there_ref = f32[2,8,512]{2,1,0:T(8,128)S(1)} collective-permute-done((f32[2,8,512]{2,1,0:T(8,128)S(1)}, f32[2,8,512]{2,1,0:T(8,128)S(1)}, u32[]{:S(2)}, u32[]{:S(2)}) %collective-permute-start.11) | collective-permute-done | bytes 32800 | tf_op jit(solution)/shard_map/ppermute | solution.py:444
  41.9 1.3 %backward.10.refs_2_ = f32[8,4096]{1,0:T(8,128)S(1)} custom-call(f32[2,8,512]{2,1,0:T(8,128)S(1)} %get-tuple-element.57.resid_ref, f32[2,8,128]{2,1,0:T(8,128)S(1)} %get-tuple-element.58.own_ref, f32[2,8,128]{2,1,0:T(8,128)S(1)} %collective-permute-done.12.other_ref, f32[2,512]{1,0:T(2,128)S(1)} %copy-done.1, s32[2,512]{1,0:T(2,128)S(1)} %copy-done, ...), custom_call_target="tpu_custom_call" | custom-call | flops 1073741824 | bytes 8388608 | tf_op jit(solution)/shard_map/backward/pallas_call | solution.py:381
  43.4 1.3 %backward.11.refs_2_ = f32[8,4096]{1,0:T(8,128)S(1)} custom-call(f32[2,8,512]{2,1,0:T(8,128)S(1)} %get-tuple-element.57.resid_ref, f32[2,8,128]{2,1,0:T(8,128)S(1)} %get-tuple-element.58.own_ref, f32[2,8,128]{2,1,0:T(8,128)S(1)} %collective-permute-done.12.other_ref, f32[2,512]{1,0:T(2,128)S(1)} %copy-done.1, s32[2,512]{1,0:T(2,128)S(1)} %copy-done, ...), custom_call_target="tpu_custom_call" | custom-call | flops 1073741824 | bytes 8388608 | tf_op jit(solution)/shard_map/backward/pallas_call | solution.py:381
  46.3 1.2 %forward.9 = (f32[8,4096]{1,0:T(8,128)S(1)}, f32[2,8,1024]{2,1,0:T(8,128)S(1)}, f32[2,8,512]{2,1,0:T(8,128)S(1)}) custom-call(f32[8,4096]{1,0:T(8,128)S(1)} %get-tuple-element.59.refs_1_.refs_0_, f32[8,4096]{1,0:T(8,128)S(1)} %get-tuple-element.48.refs_1_.refs_0_.refs_2_, f32[8,4096]{1,0:T(8,128)S(1)} %backward.11.refs_2_, ...), custom_call_target="tpu_custom_call" | custom-call | flops 1073741824 | bytes 8388608 | tf_op jit(solution)/shard_map/forward/pallas_call | solution.py:206
  47.5 2.6 %collective-permute-start.18 = (f32[2,8,512]{2,1,0:T(8,128)S(1)}, f32[2,8,512]{2,1,0:T(8,128)S(1)}, u32[]{:S(2)}, u32[]{:S(2)}) collective-permute-start(f32[2,8,512]{2,1,0:T(8,128)S(1)} %get-tuple-element.65), channel_id=1, source_target_pairs={{0,12},{2,14},{4,8},{6,10},{8,4},{10,6},{12,0},{14,2},{1,13},{3,15... | collective-permute-start | bytes 98312 | tf_op jit(solution)/shard_map/ppermute | solution.py:444
  51.9 1.3 %collective-permute-start.21 = (f32[2,8,1024]{2,1,0:T(8,128)S(1)}, f32[2,8,1024]{2,1,0:T(8,128)S(1)}, u32[]{:S(2)}, u32[]{:S(2)}) collective-permute-start(f32[2,8,1024]{2,1,0:T(8,128)S(1)} %get-tuple-element.69), channel_id=1, source_target_pairs={{2,0},{4,2},{6,4},{8,6},{10,8},{12,10},{14,12},{1,3},{3,5},{5,7},{... | collective-permute-start | bytes 196616 | tf_op jit(solution)/shard_map/ppermute | solution.py:440
  53.5 1.4 %collective-permute-done.17 = f32[2,8,512]{2,1,0:T(8,128)S(1)} collective-permute-done((f32[2,8,512]{2,1,0:T(8,128)S(1)}, f32[2,8,512]{2,1,0:T(8,128)S(1)}, u32[]{:S(2)}, u32[]{:S(2)}) %collective-permute-start.17) | collective-permute-done | bytes 32800 | tf_op jit(solution)/shard_map/ppermute | solution.py:444
  55.2 1.2 %collective-permute-start.19 = (f32[2,8,512]{2,1,0:T(8,128)S(1)}, f32[2,8,512]{2,1,0:T(8,128)S(1)}, u32[]{:S(2)}, u32[]{:S(2)}) collective-permute-start(f32[2,8,512]{2,1,0:T(8,128)S(1)} %add_add_fusion.1.here_ref), channel_id=1, source_target_pairs={{0,2},{2,0},{4,6},{6,4},{8,10},{10,8},{12,14},{14,12},{1,3},{3,1},... | collective-permute-start | bytes 98312 | tf_op jit(solution)/shard_map/ppermute | solution.py:444
  56.5 2.8 %collective-permute-done.19.there_ref = f32[2,8,512]{2,1,0:T(8,128)S(1)} collective-permute-done((f32[2,8,512]{2,1,0:T(8,128)S(1)}, f32[2,8,512]{2,1,0:T(8,128)S(1)}, u32[]{:S(2)}, u32[]{:S(2)}) %collective-permute-start.19) | collective-permute-done | bytes 32800 | tf_op jit(solution)/shard_map/ppermute | solution.py:444
  60.6 1.3 %backward.12.refs_2_ = f32[8,4096]{1,0:T(8,128)S(1)} custom-call(f32[2,8,512]{2,1,0:T(8,128)S(1)} %get-tuple-element.66.resid_ref, f32[2,8,128]{2,1,0:T(8,128)S(1)} %get-tuple-element.67.own_ref, f32[2,8,128]{2,1,0:T(8,128)S(1)} %collective-permute-done.20.other_ref, f32[2,512]{1,0:T(2,128)S(1)} %copy-done.1, s32[2,512]{1,0:T(2,128)S(1)} %copy-done, ...), custom_call_target="tpu_custom_call" | custom-call | flops 1073741824 | bytes 8388608 | tf_op jit(solution)/shard_map/backward/pallas_call | solution.py:381
  62.1 1.3 %backward.13.refs_2_ = f32[8,4096]{1,0:T(8,128)S(1)} custom-call(f32[2,8,512]{2,1,0:T(8,128)S(1)} %get-tuple-element.66.resid_ref, f32[2,8,128]{2,1,0:T(8,128)S(1)} %get-tuple-element.67.own_ref, f32[2,8,128]{2,1,0:T(8,128)S(1)} %collective-permute-done.20.other_ref, f32[2,512]{1,0:T(2,128)S(1)} %copy-done.1, s32[2,512]{1,0:T(2,128)S(1)} %copy-done, ...), custom_call_target="tpu_custom_call" | custom-call | flops 1073741824 | bytes 8388608 | tf_op jit(solution)/shard_map/backward/pallas_call | solution.py:381
  65.0 1.2 %forward.11 = (f32[8,4096]{1,0:T(8,128)S(1)}, f32[2,8,1024]{2,1,0:T(8,128)S(1)}, f32[2,8,512]{2,1,0:T(8,128)S(1)}) custom-call(f32[8,4096]{1,0:T(8,128)S(1)} %get-tuple-element.68.refs_1_.refs_0_, f32[8,4096]{1,0:T(8,128)S(1)} %get-tuple-element.48.refs_1_.refs_0_.refs_2_, f32[8,4096]{1,0:T(8,128)S(1)} %backward.13.refs_2_, ...), custom_call_target="tpu_custom_call" | custom-call | flops 1073741824 | bytes 8388608 | tf_op jit(solution)/shard_map/forward/pallas_call | solution.py:206
  66.2 2.0 %collective-permute-start.26 = (f32[2,8,512]{2,1,0:T(8,128)S(1)}, f32[2,8,512]{2,1,0:T(8,128)S(1)}, u32[]{:S(2)}, u32[]{:S(2)}) collective-permute-start(f32[2,8,512]{2,1,0:T(8,128)S(1)} %get-tuple-element.74), channel_id=1, source_target_pairs={{0,12},{2,14},{4,8},{6,10},{8,4},{10,6},{12,0},{14,2},{1,13},{3,15... | collective-permute-start | bytes 98312 | tf_op jit(solution)/shard_map/ppermute | solution.py:444
  68.1 1.6 %collective-permute-start.25 = (f32[2,8,512]{2,1,0:T(8,128)S(1)}, f32[2,8,512]{2,1,0:T(8,128)S(1)}, u32[]{:S(2)}, u32[]{:S(2)}) collective-permute-start(f32[2,8,512]{2,1,0:T(8,128)S(1)} %get-tuple-element.74), channel_id=1, source_target_pairs={{0,8},{2,10},{4,12},{6,14},{8,0},{10,2},{12,4},{14,6},{1,9},{3,11}... | collective-permute-start | bytes 98312 | tf_op jit(solution)/shard_map/ppermute | solution.py:444
  70.6 1.3 %collective-permute-start.29 = (f32[2,8,1024]{2,1,0:T(8,128)S(1)}, f32[2,8,1024]{2,1,0:T(8,128)S(1)}, u32[]{:S(2)}, u32[]{:S(2)}) collective-permute-start(f32[2,8,1024]{2,1,0:T(8,128)S(1)} %get-tuple-element.78), channel_id=1, source_target_pairs={{2,0},{4,2},{6,4},{8,6},{10,8},{12,10},{14,12},{1,3},{3,5},{5,7},{... | collective-permute-start | bytes 196616 | tf_op jit(solution)/shard_map/ppermute | solution.py:440
  73.7 1.2 %collective-permute-start.27 = (f32[2,8,512]{2,1,0:T(8,128)S(1)}, f32[2,8,512]{2,1,0:T(8,128)S(1)}, u32[]{:S(2)}, u32[]{:S(2)}) collective-permute-start(f32[2,8,512]{2,1,0:T(8,128)S(1)} %add_add_fusion.here_ref), channel_id=1, source_target_pairs={{0,2},{2,0},{4,6},{6,4},{8,10},{10,8},{12,14},{14,12},{1,3},{3,1},... | collective-permute-start | bytes 98312 | tf_op jit(solution)/shard_map/ppermute | solution.py:444
  75.0 2.7 %collective-permute-done.27.there_ref = f32[2,8,512]{2,1,0:T(8,128)S(1)} collective-permute-done((f32[2,8,512]{2,1,0:T(8,128)S(1)}, f32[2,8,512]{2,1,0:T(8,128)S(1)}, u32[]{:S(2)}, u32[]{:S(2)}) %collective-permute-start.27) | collective-permute-done | bytes 32800 | tf_op jit(solution)/shard_map/ppermute | solution.py:444
  79.0 1.3 %backward.14.own_ref = f32[8,4096]{1,0:T(8,128)S(1)} custom-call(f32[2,8,512]{2,1,0:T(8,128)S(1)} %get-tuple-element.75.resid_ref, f32[2,8,128]{2,1,0:T(8,128)S(1)} %get-tuple-element.76.own_ref, f32[2,8,128]{2,1,0:T(8,128)S(1)} %collective-permute-done.28.other_ref, f32[2,512]{1,0:T(2,128)S(1)} %copy-done.1, s32[2,512]{1,0:T(2,128)S(1)} %copy-done, ...), custom_call_target="tpu_custom_call" | custom-call | flops 1073741824 | bytes 8388608 | tf_op jit(solution)/shard_map/backward/pallas_call | solution.py:381
  80.6 1.3 %backward.15.refs_3_ = f32[8,4096]{1,0:T(8,128)S(1)} custom-call(f32[2,8,512]{2,1,0:T(8,128)S(1)} %get-tuple-element.75.resid_ref, f32[2,8,128]{2,1,0:T(8,128)S(1)} %get-tuple-element.76.own_ref, f32[2,8,128]{2,1,0:T(8,128)S(1)} %collective-permute-done.28.other_ref, f32[2,512]{1,0:T(2,128)S(1)} %copy-done.1, s32[2,512]{1,0:T(2,128)S(1)} %copy-done, ...), custom_call_target="tpu_custom_call" | custom-call | flops 1073741824 | bytes 8388608 | tf_op jit(solution)/shard_map/backward/pallas_call | solution.py:381
  (69 shorter events, 20.3 us)
Async XLA Ops:
  8.3 7.1 %collective-permute-start.2 = (f32[2,8,512]{2,1,0:T(8,128)S(1)}, f32[2,8,512]{2,1,0:T(8,128)S(1)}, u32[]{:S(2)}, u32[]{:S(2)}) collective-permute-start(f32[2,8,512]{2,1,0:T(8,128)S(1)} %get-tuple-element.44), channel_id=1, source_target_pairs={{0,12},{2,14},{4,8},{6,10},{8,4},{10,6},{12,0},{14,2},{1,13},{3,15... | collective-permute-start | bytes 98312 | tf_op jit(solution)/shard_map/ppermute | solution.py:444
  13.5 4.8 %collective-permute-start.1 = (f32[2,8,512]{2,1,0:T(8,128)S(1)}, f32[2,8,512]{2,1,0:T(8,128)S(1)}, u32[]{:S(2)}, u32[]{:S(2)}) collective-permute-start(f32[2,8,512]{2,1,0:T(8,128)S(1)} %get-tuple-element.44), channel_id=1, source_target_pairs={{0,8},{2,10},{4,12},{6,14},{8,0},{10,2},{12,4},{14,6},{1,9},{3,11}... | collective-permute-start | bytes 98312 | tf_op jit(solution)/shard_map/ppermute | solution.py:444
  13.5 4.8 %collective-permute-start = (f32[2,8,512]{2,1,0:T(8,128)S(1)}, f32[2,8,512]{2,1,0:T(8,128)S(1)}, u32[]{:S(2)}, u32[]{:S(2)}) collective-permute-start(f32[2,8,512]{2,1,0:T(8,128)S(1)} %get-tuple-element.44), channel_id=1, source_target_pairs={{0,4},{2,6},{4,0},{6,2},{8,12},{10,14},{12,8},{14,10},{1,5},{3,7},... | collective-permute-start | bytes 98312 | tf_op jit(solution)/shard_map/ppermute | solution.py:444
  14.1 8.4 %collective-permute-start.5 = (f32[2,8,1024]{2,1,0:T(8,128)S(1)}, f32[2,8,1024]{2,1,0:T(8,128)S(1)}, u32[]{:S(2)}, u32[]{:S(2)}) collective-permute-start(f32[2,8,1024]{2,1,0:T(8,128)S(1)} %get-tuple-element.49), channel_id=1, source_target_pairs={{2,0},{4,2},{6,4},{8,6},{10,8},{12,10},{14,12},{1,3},{3,5},{5,7},{... | collective-permute-start | bytes 196616 | tf_op jit(solution)/shard_map/ppermute | solution.py:440
  18.3 4.0 %collective-permute-start.3 = (f32[2,8,512]{2,1,0:T(8,128)S(1)}, f32[2,8,512]{2,1,0:T(8,128)S(1)}, u32[]{:S(2)}, u32[]{:S(2)}) collective-permute-start(f32[2,8,512]{2,1,0:T(8,128)S(1)} %add_add_fusion.3.here_ref), channel_id=1, source_target_pairs={{0,2},{2,0},{4,6},{6,4},{8,10},{10,8},{12,14},{14,12},{1,3},{3,1},... | collective-permute-start | bytes 98312 | tf_op jit(solution)/shard_map/ppermute | solution.py:444
  22.4 1.2 %collective-permute-start.4 = (f32[2,8,128]{2,1,0:T(8,128)S(1)}, f32[2,8,128]{2,1,0:T(8,128)S(1)}, u32[]{:S(2)}, u32[]{:S(2)}) collective-permute-start(f32[2,8,128]{2,1,0:T(8,128)S(1)} %get-tuple-element.47.own_ref), channel_id=1, source_target_pairs={{0,1},{1,0},{2,3},{3,2},{4,5},{5,4},{6,7},{7,6},{8,9},{9,8},{10,11... | collective-permute-start | bytes 24584 | tf_op jit(solution)/shard_map/ppermute | solution.py:433
  25.0 1.9 %collective-permute-start.6 = (f32[8,4096]{1,0:T(8,128)S(1)}, f32[8,4096]{1,0:T(8,128)S(1)}, u32[]{:S(2)}, u32[]{:S(2)}) collective-permute-start(f32[8,4096]{1,0:T(8,128)S(1)} %backward.8.refs_2_), channel_id=1, source_target_pairs={{0,1},{1,0},{2,3},{3,2},{4,5},{5,4},{6,7},{7,6},{8,9},{9,8},{10,11... | collective-permute-start | bytes 393224 | tf_op jit(solution)/shard_map/ppermute | solution.py:433
  26.5 1.5 %collective-permute-start.7 = (f32[8,4096]{1,0:T(8,128)S(1)}, f32[8,4096]{1,0:T(8,128)S(1)}, u32[]{:S(2)}, u32[]{:S(2)}) collective-permute-start(f32[8,4096]{1,0:T(8,128)S(1)} %backward.9.refs_2_), channel_id=1, source_target_pairs={{0,1},{1,0},{2,3},{3,2},{4,5},{5,4},{6,7},{7,6},{8,9},{9,8},{10,11... | collective-permute-start | bytes 393224 | tf_op jit(solution)/shard_map/ppermute | solution.py:433
  29.2 6.1 %collective-permute-start.10 = (f32[2,8,512]{2,1,0:T(8,128)S(1)}, f32[2,8,512]{2,1,0:T(8,128)S(1)}, u32[]{:S(2)}, u32[]{:S(2)}) collective-permute-start(f32[2,8,512]{2,1,0:T(8,128)S(1)} %get-tuple-element.56), channel_id=1, source_target_pairs={{0,12},{2,14},{4,8},{6,10},{8,4},{10,6},{12,0},{14,2},{1,13},{3,15... | collective-permute-start | bytes 98312 | tf_op jit(solution)/shard_map/ppermute | solution.py:444
  31.7 4.8 %collective-permute-start.9 = (f32[2,8,512]{2,1,0:T(8,128)S(1)}, f32[2,8,512]{2,1,0:T(8,128)S(1)}, u32[]{:S(2)}, u32[]{:S(2)}) collective-permute-start(f32[2,8,512]{2,1,0:T(8,128)S(1)} %get-tuple-element.56), channel_id=1, source_target_pairs={{0,8},{2,10},{4,12},{6,14},{8,0},{10,2},{12,4},{14,6},{1,9},{3,11}... | collective-permute-start | bytes 98312 | tf_op jit(solution)/shard_map/ppermute | solution.py:444
  31.7 4.8 %collective-permute-start.8 = (f32[2,8,512]{2,1,0:T(8,128)S(1)}, f32[2,8,512]{2,1,0:T(8,128)S(1)}, u32[]{:S(2)}, u32[]{:S(2)}) collective-permute-start(f32[2,8,512]{2,1,0:T(8,128)S(1)} %get-tuple-element.56), channel_id=1, source_target_pairs={{0,4},{2,6},{4,0},{6,2},{8,12},{10,14},{12,8},{14,10},{1,5},{3,7},... | collective-permute-start | bytes 98312 | tf_op jit(solution)/shard_map/ppermute | solution.py:444
  33.6 7.1 %collective-permute-start.13 = (f32[2,8,1024]{2,1,0:T(8,128)S(1)}, f32[2,8,1024]{2,1,0:T(8,128)S(1)}, u32[]{:S(2)}, u32[]{:S(2)}) collective-permute-start(f32[2,8,1024]{2,1,0:T(8,128)S(1)} %get-tuple-element.60), channel_id=1, source_target_pairs={{2,0},{4,2},{6,4},{8,6},{10,8},{12,10},{14,12},{1,3},{3,5},{5,7},{... | collective-permute-start | bytes 196616 | tf_op jit(solution)/shard_map/ppermute | solution.py:440
  36.5 4.0 %collective-permute-start.11 = (f32[2,8,512]{2,1,0:T(8,128)S(1)}, f32[2,8,512]{2,1,0:T(8,128)S(1)}, u32[]{:S(2)}, u32[]{:S(2)}) collective-permute-start(f32[2,8,512]{2,1,0:T(8,128)S(1)} %add_add_fusion.2.here_ref), channel_id=1, source_target_pairs={{0,2},{2,0},{4,6},{6,4},{8,10},{10,8},{12,14},{14,12},{1,3},{3,1},... | collective-permute-start | bytes 98312 | tf_op jit(solution)/shard_map/ppermute | solution.py:444
  40.6 1.2 %collective-permute-start.12 = (f32[2,8,128]{2,1,0:T(8,128)S(1)}, f32[2,8,128]{2,1,0:T(8,128)S(1)}, u32[]{:S(2)}, u32[]{:S(2)}) collective-permute-start(f32[2,8,128]{2,1,0:T(8,128)S(1)} %get-tuple-element.58.own_ref), channel_id=1, source_target_pairs={{0,1},{1,0},{2,3},{3,2},{4,5},{5,4},{6,7},{7,6},{8,9},{9,8},{10,11... | collective-permute-start | bytes 24584 | tf_op jit(solution)/shard_map/ppermute | solution.py:433
  43.2 1.9 %collective-permute-start.14 = (f32[8,4096]{1,0:T(8,128)S(1)}, f32[8,4096]{1,0:T(8,128)S(1)}, u32[]{:S(2)}, u32[]{:S(2)}) collective-permute-start(f32[8,4096]{1,0:T(8,128)S(1)} %backward.10.refs_2_), channel_id=1, source_target_pairs={{0,1},{1,0},{2,3},{3,2},{4,5},{5,4},{6,7},{7,6},{8,9},{9,8},{10,11... | collective-permute-start | bytes 393224 | tf_op jit(solution)/shard_map/ppermute | solution.py:433
  44.7 1.5 %collective-permute-start.15 = (f32[8,4096]{1,0:T(8,128)S(1)}, f32[8,4096]{1,0:T(8,128)S(1)}, u32[]{:S(2)}, u32[]{:S(2)}) collective-permute-start(f32[8,4096]{1,0:T(8,128)S(1)} %backward.11.refs_2_), channel_id=1, source_target_pairs={{0,1},{1,0},{2,3},{3,2},{4,5},{5,4},{6,7},{7,6},{8,9},{9,8},{10,11... | collective-permute-start | bytes 393224 | tf_op jit(solution)/shard_map/ppermute | solution.py:433
  47.5 6.1 %collective-permute-start.18 = (f32[2,8,512]{2,1,0:T(8,128)S(1)}, f32[2,8,512]{2,1,0:T(8,128)S(1)}, u32[]{:S(2)}, u32[]{:S(2)}) collective-permute-start(f32[2,8,512]{2,1,0:T(8,128)S(1)} %get-tuple-element.65), channel_id=1, source_target_pairs={{0,12},{2,14},{4,8},{6,10},{8,4},{10,6},{12,0},{14,2},{1,13},{3,15... | collective-permute-start | bytes 98312 | tf_op jit(solution)/shard_map/ppermute | solution.py:444
  50.1 4.8 %collective-permute-start.17 = (f32[2,8,512]{2,1,0:T(8,128)S(1)}, f32[2,8,512]{2,1,0:T(8,128)S(1)}, u32[]{:S(2)}, u32[]{:S(2)}) collective-permute-start(f32[2,8,512]{2,1,0:T(8,128)S(1)} %get-tuple-element.65), channel_id=1, source_target_pairs={{0,8},{2,10},{4,12},{6,14},{8,0},{10,2},{12,4},{14,6},{1,9},{3,11}... | collective-permute-start | bytes 98312 | tf_op jit(solution)/shard_map/ppermute | solution.py:444
  51.0 4.3 %collective-permute-start.16 = (f32[2,8,512]{2,1,0:T(8,128)S(1)}, f32[2,8,512]{2,1,0:T(8,128)S(1)}, u32[]{:S(2)}, u32[]{:S(2)}) collective-permute-start(f32[2,8,512]{2,1,0:T(8,128)S(1)} %get-tuple-element.65), channel_id=1, source_target_pairs={{0,4},{2,6},{4,0},{6,2},{8,12},{10,14},{12,8},{14,10},{1,5},{3,7},... | collective-permute-start | bytes 98312 | tf_op jit(solution)/shard_map/ppermute | solution.py:444
  51.9 7.5 %collective-permute-start.21 = (f32[2,8,1024]{2,1,0:T(8,128)S(1)}, f32[2,8,1024]{2,1,0:T(8,128)S(1)}, u32[]{:S(2)}, u32[]{:S(2)}) collective-permute-start(f32[2,8,1024]{2,1,0:T(8,128)S(1)} %get-tuple-element.69), channel_id=1, source_target_pairs={{2,0},{4,2},{6,4},{8,6},{10,8},{12,10},{14,12},{1,3},{3,5},{5,7},{... | collective-permute-start | bytes 196616 | tf_op jit(solution)/shard_map/ppermute | solution.py:440
  55.2 4.0 %collective-permute-start.19 = (f32[2,8,512]{2,1,0:T(8,128)S(1)}, f32[2,8,512]{2,1,0:T(8,128)S(1)}, u32[]{:S(2)}, u32[]{:S(2)}) collective-permute-start(f32[2,8,512]{2,1,0:T(8,128)S(1)} %add_add_fusion.1.here_ref), channel_id=1, source_target_pairs={{0,2},{2,0},{4,6},{6,4},{8,10},{10,8},{12,14},{14,12},{1,3},{3,1},... | collective-permute-start | bytes 98312 | tf_op jit(solution)/shard_map/ppermute | solution.py:444
  59.3 1.2 %collective-permute-start.20 = (f32[2,8,128]{2,1,0:T(8,128)S(1)}, f32[2,8,128]{2,1,0:T(8,128)S(1)}, u32[]{:S(2)}, u32[]{:S(2)}) collective-permute-start(f32[2,8,128]{2,1,0:T(8,128)S(1)} %get-tuple-element.67.own_ref), channel_id=1, source_target_pairs={{0,1},{1,0},{2,3},{3,2},{4,5},{5,4},{6,7},{7,6},{8,9},{9,8},{10,11... | collective-permute-start | bytes 24584 | tf_op jit(solution)/shard_map/ppermute | solution.py:433
  61.9 1.9 %collective-permute-start.22 = (f32[8,4096]{1,0:T(8,128)S(1)}, f32[8,4096]{1,0:T(8,128)S(1)}, u32[]{:S(2)}, u32[]{:S(2)}) collective-permute-start(f32[8,4096]{1,0:T(8,128)S(1)} %backward.12.refs_2_), channel_id=1, source_target_pairs={{0,1},{1,0},{2,3},{3,2},{4,5},{5,4},{6,7},{7,6},{8,9},{9,8},{10,11... | collective-permute-start | bytes 393224 | tf_op jit(solution)/shard_map/ppermute | solution.py:433
  63.4 1.5 %collective-permute-start.23 = (f32[8,4096]{1,0:T(8,128)S(1)}, f32[8,4096]{1,0:T(8,128)S(1)}, u32[]{:S(2)}, u32[]{:S(2)}) collective-permute-start(f32[8,4096]{1,0:T(8,128)S(1)} %backward.13.refs_2_), channel_id=1, source_target_pairs={{0,1},{1,0},{2,3},{3,2},{4,5},{5,4},{6,7},{7,6},{8,9},{9,8},{10,11... | collective-permute-start | bytes 393224 | tf_op jit(solution)/shard_map/ppermute | solution.py:433
  66.2 6.0 %collective-permute-start.26 = (f32[2,8,512]{2,1,0:T(8,128)S(1)}, f32[2,8,512]{2,1,0:T(8,128)S(1)}, u32[]{:S(2)}, u32[]{:S(2)}) collective-permute-start(f32[2,8,512]{2,1,0:T(8,128)S(1)} %get-tuple-element.74), channel_id=1, source_target_pairs={{0,12},{2,14},{4,8},{6,10},{8,4},{10,6},{12,0},{14,2},{1,13},{3,15... | collective-permute-start | bytes 98312 | tf_op jit(solution)/shard_map/ppermute | solution.py:444
  68.1 5.2 %collective-permute-start.25 = (f32[2,8,512]{2,1,0:T(8,128)S(1)}, f32[2,8,512]{2,1,0:T(8,128)S(1)}, u32[]{:S(2)}, u32[]{:S(2)}) collective-permute-start(f32[2,8,512]{2,1,0:T(8,128)S(1)} %get-tuple-element.74), channel_id=1, source_target_pairs={{0,8},{2,10},{4,12},{6,14},{8,0},{10,2},{12,4},{14,6},{1,9},{3,11}... | collective-permute-start | bytes 98312 | tf_op jit(solution)/shard_map/ppermute | solution.py:444
  69.7 4.0 %collective-permute-start.24 = (f32[2,8,512]{2,1,0:T(8,128)S(1)}, f32[2,8,512]{2,1,0:T(8,128)S(1)}, u32[]{:S(2)}, u32[]{:S(2)}) collective-permute-start(f32[2,8,512]{2,1,0:T(8,128)S(1)} %get-tuple-element.74), channel_id=1, source_target_pairs={{0,4},{2,6},{4,0},{6,2},{8,12},{10,14},{12,8},{14,10},{1,5},{3,7},... | collective-permute-start | bytes 98312 | tf_op jit(solution)/shard_map/ppermute | solution.py:444
  70.6 7.3 %collective-permute-start.29 = (f32[2,8,1024]{2,1,0:T(8,128)S(1)}, f32[2,8,1024]{2,1,0:T(8,128)S(1)}, u32[]{:S(2)}, u32[]{:S(2)}) collective-permute-start(f32[2,8,1024]{2,1,0:T(8,128)S(1)} %get-tuple-element.78), channel_id=1, source_target_pairs={{2,0},{4,2},{6,4},{8,6},{10,8},{12,10},{14,12},{1,3},{3,5},{5,7},{... | collective-permute-start | bytes 196616 | tf_op jit(solution)/shard_map/ppermute | solution.py:440
  73.7 4.0 %collective-permute-start.27 = (f32[2,8,512]{2,1,0:T(8,128)S(1)}, f32[2,8,512]{2,1,0:T(8,128)S(1)}, u32[]{:S(2)}, u32[]{:S(2)}) collective-permute-start(f32[2,8,512]{2,1,0:T(8,128)S(1)} %add_add_fusion.here_ref), channel_id=1, source_target_pairs={{0,2},{2,0},{4,6},{6,4},{8,10},{10,8},{12,14},{14,12},{1,3},{3,1},... | collective-permute-start | bytes 98312 | tf_op jit(solution)/shard_map/ppermute | solution.py:444
  77.8 1.2 %collective-permute-start.28 = (f32[2,8,128]{2,1,0:T(8,128)S(1)}, f32[2,8,128]{2,1,0:T(8,128)S(1)}, u32[]{:S(2)}, u32[]{:S(2)}) collective-permute-start(f32[2,8,128]{2,1,0:T(8,128)S(1)} %get-tuple-element.76.own_ref), channel_id=1, source_target_pairs={{0,1},{1,0},{2,3},{3,2},{4,5},{5,4},{6,7},{7,6},{8,9},{9,8},{10,11... | collective-permute-start | bytes 24584 | tf_op jit(solution)/shard_map/ppermute | solution.py:433
  80.4 1.9 %collective-permute-start.30 = (f32[8,4096]{1,0:T(8,128)S(1)}, f32[8,4096]{1,0:T(8,128)S(1)}, u32[]{:S(2)}, u32[]{:S(2)}) collective-permute-start(f32[8,4096]{1,0:T(8,128)S(1)} %backward.14.own_ref), channel_id=1, source_target_pairs={{0,1},{1,0},{2,3},{3,2},{4,5},{5,4},{6,7},{7,6},{8,9},{9,8},{10,11... | collective-permute-start | bytes 393224 | tf_op jit(solution)/shard_map/ppermute | solution.py:433
  81.9 1.4 %collective-permute-start.31 = (f32[8,4096]{1,0:T(8,128)S(1)}, f32[8,4096]{1,0:T(8,128)S(1)}, u32[]{:S(2)}, u32[]{:S(2)}) collective-permute-start(f32[8,4096]{1,0:T(8,128)S(1)} %backward.15.refs_3_), channel_id=1, source_target_pairs={{0,1},{1,0},{2,3},{3,2},{4,5},{5,4},{6,7},{7,6},{8,9},{9,8},{10,11... | collective-permute-start | bytes 393224 | tf_op jit(solution)/shard_map/ppermute | solution.py:433
  (4 other events, 89.1 us)
where the time goes:
time: 84.2 us; the launch traced here: 84 us
  starting transfers between devices  32.1 us (38%)
  Pallas kernels  28.9 us (34%)
  waiting for transfers between devices  22.8 us (27%)
    ppermute x16, starting transfers between devices, fetch(): return lax.ppermute(values, 'cell', [(i, i ^ by) for i in range(devices)])  24.5 us
    ppermute x16, waiting for transfers between devices, fetch(): return lax.ppermute(values, 'cell', [(i, i ^ by) for i in range(devices)])  18.8 us
    pallas_call x8, Pallas kernels, backward(): pl.pallas_call(functools.partial(backward_kernel, survey), out_shape=jax....  10.6 us
    pallas_call x1, Pallas kernels, prepare(): pl.pallas_call(functools.partial(prepare_kernel, block), out_shape=[pltpu...  8.31 us
    pallas_call x6, Pallas kernels, forward(): pl.pallas_call(functools.partial(forward_kernel, survey), out_shape=out_s...  7.13 us
    ppermute x4, starting transfers between devices, exchange_edges(): return lax.ppermute(edge, ('cell', 'dp'), pairs)  5.12 us
    ppermute x12, waiting for transfers between devices, from_pair(): return lax.ppermute(values, 'dp', [(0, 1), (1, 0)])  3.95 us
    ppermute x12, starting transfers between devices, from_pair(): return lax.ppermute(values, 'dp', [(0, 1), (1, 0)])  2.45 us
  transfers between devices with their start and end apart: 32, of which 18 were waited for; matrix products, arithmetic and copies ran while one was open for 0% of the time, Pallas kernels for 13%

commit v1 on v0

--- a/solution.py
+++ b/solution.py
@@ -83,12 +83,12 @@
     prior_copy.wait()
     for step in range(min(2, ahead), ahead):
         copy(step).start()
-    upward = lax.axis_index("dp") == 0
+    downward = lax.axis_index("dp") == 0
     for survey in range(surveys):
         layer_rows = [prior_buffer[survey, :, at, :] for at in range(layers)]
         for at in range(layers):
             flat_refs[survey][:, at * layer_cells : (at + 1) * layer_cells] = layer_rows[at]
-        edge_ref[survey] = jnp.where(upward, layer_rows[0], layer_rows[-1])
+        edge_ref[survey] = jnp.where(downward, layer_rows[-1], layer_rows[0])
     ids_copy.wait()
     lane = lax.broadcasted_iota(jnp.int32, (model_count, LANES), 1)
     for survey in range(surveys):
@@ -179,10 +179,10 @@
         part_ref[at] = earlier_parts[at][...]
     cells = models.shape[1]
     layer_cells = edge_ref.shape[2]
-    upward = lax.axis_index("dp") == 0
+    downward = lax.axis_index("dp") == 0
     for at, ref in enumerate((*earlier_models, next_ref)):
         edge_ref[at] = jnp.where(
-            upward, ref[:, :layer_cells], ref[:, cells - layer_cells :]
+            downward, ref[:, cells - layer_cells :], ref[:, :layer_cells]
         )
 
 
@@ -435,8 +435,8 @@
 
 def exchange_edges(edge):
     devices = lax.axis_size("cell")
-    pairs = [(2 * i, 2 * i - 2) for i in range(1, devices)]
-    pairs += [(2 * i + 1, 2 * i + 3) for i in range(devices - 1)]
+    pairs = [(2 * i, 2 * i + 3) for i in range(devices - 1)]
+    pairs += [(2 * i + 3, 2 * i) for i in range(devices - 1)]
     return lax.ppermute(edge, ("cell", "dp"), pairs)
 
 

time: 84.2 us -> 83.1 us (0.987)
  waiting for transfers between devices: 22.8 us -> 17 us
  starting transfers between devices: 32.1 us -> 36.7 us
    ppermute x16, waiting for transfers between devices: 18.8 us -> 13 us  [fetch(): return lax.ppermute(values, 'cell', [(i, i ^ by) for i in range(devices)])]
    ppermute x4, starting transfers between devices: 5.12 us -> 9.57 us  [exchange_edges(): return lax.ppermute(edge, ('cell', 'dp'), pairs)]
  transfers between devices with their start and end apart: 32 -> 32, of which waited for: 18 -> 13; matrix products, arithmetic and copies ran while one was open for 0% -> 0% of each run, Pallas kernels for 13% -> 13%
where the time goes in v1:
time: 83.1 us; the launch traced here: 82.9 us
  starting transfers between devices  36.7 us (44%)
  Pallas kernels  28.9 us (35%)
  waiting for transfers between devices  17 us (20%)
    ppermute x16, starting transfers between devices, fetch(): return lax.ppermute(values, 'cell', [(i, i ^ by) for i in range(devices)])  24.7 us
    ppermute x16, waiting for transfers between devices, fetch(): return lax.ppermute(values, 'cell', [(i, i ^ by) for i in range(devices)])  13 us
    pallas_call x8, Pallas kernels, backward(): pl.pallas_call(functools.partial(backward_kernel, survey), out_shape=jax....  10.6 us
    ppermute x4, starting transfers between devices, exchange_edges(): return lax.ppermute(edge, ('cell', 'dp'), pairs)  9.57 us
    pallas_call x1, Pallas kernels, prepare(): pl.pallas_call(functools.partial(prepare_kernel, block), out_shape=[pltpu...  8.31 us
    pallas_call x6, Pallas kernels, forward(): pl.pallas_call(functools.partial(forward_kernel, survey), out_shape=out_s...  7.13 us
    ppermute x12, waiting for transfers between devices, from_pair(): return lax.ppermute(values, 'dp', [(0, 1), (1, 0)])  3.95 us
    ppermute x12, starting transfers between devices, from_pair(): return lax.ppermute(values, 'dp', [(0, 1), (1, 0)])  2.45 us
  transfers between devices with their start and end apart: 32, of which 13 were waited for; matrix products, arithmetic and copies ran while one was open for 0% of the time, Pallas kernels for 13%

profile of v1, /device:TPU:0, one launch (start us, length us, event | category | flops | bytes accessed | tf_op | source)
XLA Modules:
  0.0 82.9 jit_solution(9856103688533690504)
XLA Ops:
  0.0 8.3 %prepare.1 = (bf16[2,2,512,4096]{3,2,1,0:T(8,128)(2,1)S(1)}, bf16[2,2,4096,512]{3,2,1,0:T(8,128)(2,1)S(1)}, f32[2,8,512]{2,1,0:T(8,128)S(1)}, f32[2,8,128]{2,1,0...) custom-call(f32[2,512,4096]{2,1,0:T(8,128)} %sens_ref.1, ...), custom_call_target="tpu_custom_call" | custom-call | tf_op jit(solution)/shard_map/prepare/pallas_call | solution.py:133
  8.3 5.1 %collective-permute-start.2 = (f32[2,8,512]{2,1,0:T(8,128)S(1)}, f32[2,8,512]{2,1,0:T(8,128)S(1)}, u32[]{:S(2)}, u32[]{:S(2)}) collective-permute-start(f32[2,8,512]{2,1,0:T(8,128)S(1)} %get-tuple-element.44), channel_id=1, source_target_pairs={{0,12},{2,14},{4,8},{6,10},{8,4},{10,6},{12,0},{14,2},{1,13},{3,15... | collective-permute-start | bytes 98312 | tf_op jit(solution)/shard_map/ppermute | solution.py:444
  14.1 2.3 %collective-permute-start.5 = (f32[2,8,1024]{2,1,0:T(8,128)S(1)}, f32[2,8,1024]{2,1,0:T(8,128)S(1)}, u32[]{:S(2)}, u32[]{:S(2)}) collective-permute-start(f32[2,8,1024]{2,1,0:T(8,128)S(1)} %get-tuple-element.49), channel_id=1, source_target_pairs={{0,3},{2,5},{4,7},{6,9},{8,11},{10,13},{12,15},{3,0},{5,2},{7,4},{... | collective-permute-start | bytes 196616 | tf_op jit(solution)/shard_map/ppermute | solution.py:440
  16.4 1.9 %collective-permute-done.1 = f32[2,8,512]{2,1,0:T(8,128)S(1)} collective-permute-done((f32[2,8,512]{2,1,0:T(8,128)S(1)}, f32[2,8,512]{2,1,0:T(8,128)S(1)}, u32[]{:S(2)}, u32[]{:S(2)}) %collective-permute-start.1) | collective-permute-done | bytes 32800 | tf_op jit(solution)/shard_map/ppermute | solution.py:444
  18.3 1.6 %collective-permute-start.3 = (f32[2,8,512]{2,1,0:T(8,128)S(1)}, f32[2,8,512]{2,1,0:T(8,128)S(1)}, u32[]{:S(2)}, u32[]{:S(2)}) collective-permute-start(f32[2,8,512]{2,1,0:T(8,128)S(1)} %add_add_fusion.3.here_ref), channel_id=1, source_target_pairs={{0,2},{2,0},{4,6},{6,4},{8,10},{10,8},{12,14},{14,12},{1,3},{3,1},... | collective-permute-start | bytes 98312 | tf_op jit(solution)/shard_map/ppermute | solution.py:444
  19.9 2.4 %collective-permute-done.3.there_ref = f32[2,8,512]{2,1,0:T(8,128)S(1)} collective-permute-done((f32[2,8,512]{2,1,0:T(8,128)S(1)}, f32[2,8,512]{2,1,0:T(8,128)S(1)}, u32[]{:S(2)}, u32[]{:S(2)}) %collective-permute-start.3) | collective-permute-done | bytes 32800 | tf_op jit(solution)/shard_map/ppermute | solution.py:444
  23.6 1.3 %backward.8.refs_2_ = f32[8,4096]{1,0:T(8,128)S(1)} custom-call(f32[2,8,512]{2,1,0:T(8,128)S(1)} %get-tuple-element.46.resid_ref, f32[2,8,128]{2,1,0:T(8,128)S(1)} %get-tuple-element.47.own_ref, f32[2,8,128]{2,1,0:T(8,128)S(1)} %collective-permute-done.4.other_ref, f32[2,512]{1,0:T(2,128)S(1)} %copy-done.1, s32[2,512]{1,0:T(2,128)S(1)} %copy-done, ...), custom_call_target="tpu_custom_call" | custom-call | flops 1073741824 | bytes 8388608 | tf_op jit(solution)/shard_map/backward/pallas_call | solution.py:381
  25.1 1.3 %backward.9.refs_2_ = f32[8,4096]{1,0:T(8,128)S(1)} custom-call(f32[2,8,512]{2,1,0:T(8,128)S(1)} %get-tuple-element.46.resid_ref, f32[2,8,128]{2,1,0:T(8,128)S(1)} %get-tuple-element.47.own_ref, f32[2,8,128]{2,1,0:T(8,128)S(1)} %collective-permute-done.4.other_ref, f32[2,512]{1,0:T(2,128)S(1)} %copy-done.1, s32[2,512]{1,0:T(2,128)S(1)} %copy-done, ...), custom_call_target="tpu_custom_call" | custom-call | flops 1073741824 | bytes 8388608 | tf_op jit(solution)/shard_map/backward/pallas_call | solution.py:381
  28.0 1.2 %forward.7 = (f32[8,4096]{1,0:T(8,128)S(1)}, f32[2,8,1024]{2,1,0:T(8,128)S(1)}, f32[2,8,512]{2,1,0:T(8,128)S(1)}) custom-call(f32[8,4096]{1,0:T(8,128)S(1)} %get-tuple-element.48.refs_1_.refs_0_.refs_2_, f32[8,4096]{1,0:T(8,128)S(1)} %get-tuple-element.48.refs_1_.refs_0_.refs_2_, f32[8,4096]{1,0:T(8,128)S(1)} %backward.9.refs_2_, ...), custom_call_target="tpu_custom_call" | custom-call | flops 1073741824 | bytes 8388608 | tf_op jit(solution)/shard_map/forward/pallas_call | solution.py:206
  29.2 2.0 %collective-permute-start.10 = (f32[2,8,512]{2,1,0:T(8,128)S(1)}, f32[2,8,512]{2,1,0:T(8,128)S(1)}, u32[]{:S(2)}, u32[]{:S(2)}) collective-permute-start(f32[2,8,512]{2,1,0:T(8,128)S(1)} %get-tuple-element.56), channel_id=1, source_target_pairs={{0,12},{2,14},{4,8},{6,10},{8,4},{10,6},{12,0},{14,2},{1,13},{3,15... | collective-permute-start | bytes 98312 | tf_op jit(solution)/shard_map/ppermute | solution.py:444
  31.3 2.3 %collective-permute-start.8 = (f32[2,8,512]{2,1,0:T(8,128)S(1)}, f32[2,8,512]{2,1,0:T(8,128)S(1)}, u32[]{:S(2)}, u32[]{:S(2)}) collective-permute-start(f32[2,8,512]{2,1,0:T(8,128)S(1)} %get-tuple-element.56), channel_id=1, source_target_pairs={{0,4},{2,6},{4,0},{6,2},{8,12},{10,14},{12,8},{14,10},{1,5},{3,7},... | collective-permute-start | bytes 98312 | tf_op jit(solution)/shard_map/ppermute | solution.py:444
  33.6 2.3 %collective-permute-start.13 = (f32[2,8,1024]{2,1,0:T(8,128)S(1)}, f32[2,8,1024]{2,1,0:T(8,128)S(1)}, u32[]{:S(2)}, u32[]{:S(2)}) collective-permute-start(f32[2,8,1024]{2,1,0:T(8,128)S(1)} %get-tuple-element.60), channel_id=1, source_target_pairs={{0,3},{2,5},{4,7},{6,9},{8,11},{10,13},{12,15},{3,0},{5,2},{7,4},{... | collective-permute-start | bytes 196616 | tf_op jit(solution)/shard_map/ppermute | solution.py:440
  37.5 2.9 %collective-permute-done.11.there_ref = f32[2,8,512]{2,1,0:T(8,128)S(1)} collective-permute-done((f32[2,8,512]{2,1,0:T(8,128)S(1)}, f32[2,8,512]{2,1,0:T(8,128)S(1)}, u32[]{:S(2)}, u32[]{:S(2)}) %collective-permute-start.11) | collective-permute-done | bytes 32800 | tf_op jit(solution)/shard_map/ppermute | solution.py:444
  41.8 1.3 %backward.10.refs_2_ = f32[8,4096]{1,0:T(8,128)S(1)} custom-call(f32[2,8,512]{2,1,0:T(8,128)S(1)} %get-tuple-element.57.resid_ref, f32[2,8,128]{2,1,0:T(8,128)S(1)} %get-tuple-element.58.own_ref, f32[2,8,128]{2,1,0:T(8,128)S(1)} %collective-permute-done.12.other_ref, f32[2,512]{1,0:T(2,128)S(1)} %copy-done.1, s32[2,512]{1,0:T(2,128)S(1)} %copy-done, ...), custom_call_target="tpu_custom_call" | custom-call | flops 1073741824 | bytes 8388608 | tf_op jit(solution)/shard_map/backward/pallas_call | solution.py:381
  43.3 1.3 %backward.11.refs_2_ = f32[8,4096]{1,0:T(8,128)S(1)} custom-call(f32[2,8,512]{2,1,0:T(8,128)S(1)} %get-tuple-element.57.resid_ref, f32[2,8,128]{2,1,0:T(8,128)S(1)} %get-tuple-element.58.own_ref, f32[2,8,128]{2,1,0:T(8,128)S(1)} %collective-permute-done.12.other_ref, f32[2,512]{1,0:T(2,128)S(1)} %copy-done.1, s32[2,512]{1,0:T(2,128)S(1)} %copy-done, ...), custom_call_target="tpu_custom_call" | custom-call | flops 1073741824 | bytes 8388608 | tf_op jit(solution)/shard_map/backward/pallas_call | solution.py:381
  45.0 1.2 %forward.8 = (f32[8,4096]{1,0:T(8,128)S(1)}, f32[8,512]{1,0:T(8,128)S(1)}) custom-call(f32[8,4096]{1,0:T(8,128)S(1)} %get-tuple-element.53.refs_5_.refs_0_, f32[8,4096]{1,0:T(8,128)S(1)} %get-tuple-element.43.refs_0_.refs_1_.prior_ref, f32[8,4096]{1,0:T(8,128)S(1)} %backward.10.refs_2_, f32[8,4096]{1,0:T(8,128)S(1)} %collective-permute-done.14.refs_3_, ...), custom_call_target="tpu_custom_call" | custom-call | flops 1073741824 | bytes 8388608 | tf_op jit(solution)/shard_map/forward/pallas_call | solution.py:206
  46.2 1.2 %forward.9 = (f32[8,4096]{1,0:T(8,128)S(1)}, f32[2,8,1024]{2,1,0:T(8,128)S(1)}, f32[2,8,512]{2,1,0:T(8,128)S(1)}) custom-call(f32[8,4096]{1,0:T(8,128)S(1)} %get-tuple-element.59.refs_1_.refs_0_, f32[8,4096]{1,0:T(8,128)S(1)} %get-tuple-element.48.refs_1_.refs_0_.refs_2_, f32[8,4096]{1,0:T(8,128)S(1)} %backward.11.refs_2_, ...), custom_call_target="tpu_custom_call" | custom-call | flops 1073741824 | bytes 8388608 | tf_op jit(solution)/shard_map/forward/pallas_call | solution.py:206
  47.4 2.2 %collective-permute-start.18 = (f32[2,8,512]{2,1,0:T(8,128)S(1)}, f32[2,8,512]{2,1,0:T(8,128)S(1)}, u32[]{:S(2)}, u32[]{:S(2)}) collective-permute-start(f32[2,8,512]{2,1,0:T(8,128)S(1)} %get-tuple-element.65), channel_id=1, source_target_pairs={{0,12},{2,14},{4,8},{6,10},{8,4},{10,6},{12,0},{14,2},{1,13},{3,15... | collective-permute-start | bytes 98312 | tf_op jit(solution)/shard_map/ppermute | solution.py:444
  50.1 1.6 %collective-permute-start.16 = (f32[2,8,512]{2,1,0:T(8,128)S(1)}, f32[2,8,512]{2,1,0:T(8,128)S(1)}, u32[]{:S(2)}, u32[]{:S(2)}) collective-permute-start(f32[2,8,512]{2,1,0:T(8,128)S(1)} %get-tuple-element.65), channel_id=1, source_target_pairs={{0,4},{2,6},{4,0},{6,2},{8,12},{10,14},{12,8},{14,10},{1,5},{3,7},... | collective-permute-start | bytes 98312 | tf_op jit(solution)/shard_map/ppermute | solution.py:444
  51.8 2.4 %collective-permute-start.21 = (f32[2,8,1024]{2,1,0:T(8,128)S(1)}, f32[2,8,1024]{2,1,0:T(8,128)S(1)}, u32[]{:S(2)}, u32[]{:S(2)}) collective-permute-start(f32[2,8,1024]{2,1,0:T(8,128)S(1)} %get-tuple-element.69), channel_id=1, source_target_pairs={{0,3},{2,5},{4,7},{6,9},{8,11},{10,13},{12,15},{3,0},{5,2},{7,4},{... | collective-permute-start | bytes 196616 | tf_op jit(solution)/shard_map/ppermute | solution.py:440
  54.4 1.6 %collective-permute-start.19 = (f32[2,8,512]{2,1,0:T(8,128)S(1)}, f32[2,8,512]{2,1,0:T(8,128)S(1)}, u32[]{:S(2)}, u32[]{:S(2)}) collective-permute-start(f32[2,8,512]{2,1,0:T(8,128)S(1)} %add_add_fusion.1.here_ref), channel_id=1, source_target_pairs={{0,2},{2,0},{4,6},{6,4},{8,10},{10,8},{12,14},{14,12},{1,3},{3,1},... | collective-permute-start | bytes 98312 | tf_op jit(solution)/shard_map/ppermute | solution.py:444
  56.0 2.4 %collective-permute-done.19.there_ref = f32[2,8,512]{2,1,0:T(8,128)S(1)} collective-permute-done((f32[2,8,512]{2,1,0:T(8,128)S(1)}, f32[2,8,512]{2,1,0:T(8,128)S(1)}, u32[]{:S(2)}, u32[]{:S(2)}) %collective-permute-start.19) | collective-permute-done | bytes 32800 | tf_op jit(solution)/shard_map/ppermute | solution.py:444
  59.8 1.3 %backward.12.refs_2_ = f32[8,4096]{1,0:T(8,128)S(1)} custom-call(f32[2,8,512]{2,1,0:T(8,128)S(1)} %get-tuple-element.66.resid_ref, f32[2,8,128]{2,1,0:T(8,128)S(1)} %get-tuple-element.67.own_ref, f32[2,8,128]{2,1,0:T(8,128)S(1)} %collective-permute-done.20.other_ref, f32[2,512]{1,0:T(2,128)S(1)} %copy-done.1, s32[2,512]{1,0:T(2,128)S(1)} %copy-done, ...), custom_call_target="tpu_custom_call" | custom-call | flops 1073741824 | bytes 8388608 | tf_op jit(solution)/shard_map/backward/pallas_call | solution.py:381
  61.3 1.3 %backward.13.refs_2_ = f32[8,4096]{1,0:T(8,128)S(1)} custom-call(f32[2,8,512]{2,1,0:T(8,128)S(1)} %get-tuple-element.66.resid_ref, f32[2,8,128]{2,1,0:T(8,128)S(1)} %get-tuple-element.67.own_ref, f32[2,8,128]{2,1,0:T(8,128)S(1)} %collective-permute-done.20.other_ref, f32[2,512]{1,0:T(2,128)S(1)} %copy-done.1, s32[2,512]{1,0:T(2,128)S(1)} %copy-done, ...), custom_call_target="tpu_custom_call" | custom-call | flops 1073741824 | bytes 8388608 | tf_op jit(solution)/shard_map/backward/pallas_call | solution.py:381
  64.1 1.2 %forward.11 = (f32[8,4096]{1,0:T(8,128)S(1)}, f32[2,8,1024]{2,1,0:T(8,128)S(1)}, f32[2,8,512]{2,1,0:T(8,128)S(1)}) custom-call(f32[8,4096]{1,0:T(8,128)S(1)} %get-tuple-element.68.refs_1_.refs_0_, f32[8,4096]{1,0:T(8,128)S(1)} %get-tuple-element.48.refs_1_.refs_0_.refs_2_, f32[8,4096]{1,0:T(8,128)S(1)} %backward.13.refs_2_, ...), custom_call_target="tpu_custom_call" | custom-call | flops 1073741824 | bytes 8388608 | tf_op jit(solution)/shard_map/forward/pallas_call | solution.py:206
  65.3 2.4 %collective-permute-start.26 = (f32[2,8,512]{2,1,0:T(8,128)S(1)}, f32[2,8,512]{2,1,0:T(8,128)S(1)}, u32[]{:S(2)}, u32[]{:S(2)}) collective-permute-start(f32[2,8,512]{2,1,0:T(8,128)S(1)} %get-tuple-element.74), channel_id=1, source_target_pairs={{0,12},{2,14},{4,8},{6,10},{8,4},{10,6},{12,0},{14,2},{1,13},{3,15... | collective-permute-start | bytes 98312 | tf_op jit(solution)/shard_map/ppermute | solution.py:444
  68.3 1.5 %collective-permute-start.24 = (f32[2,8,512]{2,1,0:T(8,128)S(1)}, f32[2,8,512]{2,1,0:T(8,128)S(1)}, u32[]{:S(2)}, u32[]{:S(2)}) collective-permute-start(f32[2,8,512]{2,1,0:T(8,128)S(1)} %get-tuple-element.74), channel_id=1, source_target_pairs={{0,4},{2,6},{4,0},{6,2},{8,12},{10,14},{12,8},{14,10},{1,5},{3,7},... | collective-permute-start | bytes 98312 | tf_op jit(solution)/shard_map/ppermute | solution.py:444
  69.7 2.6 %collective-permute-start.29 = (f32[2,8,1024]{2,1,0:T(8,128)S(1)}, f32[2,8,1024]{2,1,0:T(8,128)S(1)}, u32[]{:S(2)}, u32[]{:S(2)}) collective-permute-start(f32[2,8,1024]{2,1,0:T(8,128)S(1)} %get-tuple-element.78), channel_id=1, source_target_pairs={{0,3},{2,5},{4,7},{6,9},{8,11},{10,13},{12,15},{3,0},{5,2},{7,4},{... | collective-permute-start | bytes 196616 | tf_op jit(solution)/shard_map/ppermute | solution.py:440
  72.6 1.5 %collective-permute-start.27 = (f32[2,8,512]{2,1,0:T(8,128)S(1)}, f32[2,8,512]{2,1,0:T(8,128)S(1)}, u32[]{:S(2)}, u32[]{:S(2)}) collective-permute-start(f32[2,8,512]{2,1,0:T(8,128)S(1)} %add_add_fusion.here_ref), channel_id=1, source_target_pairs={{0,2},{2,0},{4,6},{6,4},{8,10},{10,8},{12,14},{14,12},{1,3},{3,1},... | collective-permute-start | bytes 98312 | tf_op jit(solution)/shard_map/ppermute | solution.py:444
  74.0 2.5 %collective-permute-done.27.there_ref = f32[2,8,512]{2,1,0:T(8,128)S(1)} collective-permute-done((f32[2,8,512]{2,1,0:T(8,128)S(1)}, f32[2,8,512]{2,1,0:T(8,128)S(1)}, u32[]{:S(2)}, u32[]{:S(2)}) %collective-permute-start.27) | collective-permute-done | bytes 32800 | tf_op jit(solution)/shard_map/ppermute | solution.py:444
  77.9 1.3 %backward.14.own_ref = f32[8,4096]{1,0:T(8,128)S(1)} custom-call(f32[2,8,512]{2,1,0:T(8,128)S(1)} %get-tuple-element.75.resid_ref, f32[2,8,128]{2,1,0:T(8,128)S(1)} %get-tuple-element.76.own_ref, f32[2,8,128]{2,1,0:T(8,128)S(1)} %collective-permute-done.28.other_ref, f32[2,512]{1,0:T(2,128)S(1)} %copy-done.1, s32[2,512]{1,0:T(2,128)S(1)} %copy-done, ...), custom_call_target="tpu_custom_call" | custom-call | flops 1073741824 | bytes 8388608 | tf_op jit(solution)/shard_map/backward/pallas_call | solution.py:381
  79.4 1.3 %backward.15.refs_3_ = f32[8,4096]{1,0:T(8,128)S(1)} custom-call(f32[2,8,512]{2,1,0:T(8,128)S(1)} %get-tuple-element.75.resid_ref, f32[2,8,128]{2,1,0:T(8,128)S(1)} %get-tuple-element.76.own_ref, f32[2,8,128]{2,1,0:T(8,128)S(1)} %collective-permute-done.28.other_ref, f32[2,512]{1,0:T(2,128)S(1)} %copy-done.1, s32[2,512]{1,0:T(2,128)S(1)} %copy-done, ...), custom_call_target="tpu_custom_call" | custom-call | flops 1073741824 | bytes 8388608 | tf_op jit(solution)/shard_map/backward/pallas_call | solution.py:381
  (69 shorter events, 15.5 us)
Async XLA Ops:
  8.3 8.1 %collective-permute-start.2 = (f32[2,8,512]{2,1,0:T(8,128)S(1)}, f32[2,8,512]{2,1,0:T(8,128)S(1)}, u32[]{:S(2)}, u32[]{:S(2)}) collective-permute-start(f32[2,8,512]{2,1,0:T(8,128)S(1)} %get-tuple-element.44), channel_id=1, source_target_pairs={{0,12},{2,14},{4,8},{6,10},{8,4},{10,6},{12,0},{14,2},{1,13},{3,15... | collective-permute-start | bytes 98312 | tf_op jit(solution)/shard_map/ppermute | solution.py:444
  13.5 4.8 %collective-permute-start.1 = (f32[2,8,512]{2,1,0:T(8,128)S(1)}, f32[2,8,512]{2,1,0:T(8,128)S(1)}, u32[]{:S(2)}, u32[]{:S(2)}) collective-permute-start(f32[2,8,512]{2,1,0:T(8,128)S(1)} %get-tuple-element.44), channel_id=1, source_target_pairs={{0,8},{2,10},{4,12},{6,14},{8,0},{10,2},{12,4},{14,6},{1,9},{3,11}... | collective-permute-start | bytes 98312 | tf_op jit(solution)/shard_map/ppermute | solution.py:444
  13.5 4.8 %collective-permute-start = (f32[2,8,512]{2,1,0:T(8,128)S(1)}, f32[2,8,512]{2,1,0:T(8,128)S(1)}, u32[]{:S(2)}, u32[]{:S(2)}) collective-permute-start(f32[2,8,512]{2,1,0:T(8,128)S(1)} %get-tuple-element.44), channel_id=1, source_target_pairs={{0,4},{2,6},{4,0},{6,2},{8,12},{10,14},{12,8},{14,10},{1,5},{3,7},... | collective-permute-start | bytes 98312 | tf_op jit(solution)/shard_map/ppermute | solution.py:444
  14.1 8.4 %collective-permute-start.5 = (f32[2,8,1024]{2,1,0:T(8,128)S(1)}, f32[2,8,1024]{2,1,0:T(8,128)S(1)}, u32[]{:S(2)}, u32[]{:S(2)}) collective-permute-start(f32[2,8,1024]{2,1,0:T(8,128)S(1)} %get-tuple-element.49), channel_id=1, source_target_pairs={{0,3},{2,5},{4,7},{6,9},{8,11},{10,13},{12,15},{3,0},{5,2},{7,4},{... | collective-permute-start | bytes 196616 | tf_op jit(solution)/shard_map/ppermute | solution.py:440
  18.3 4.0 %collective-permute-start.3 = (f32[2,8,512]{2,1,0:T(8,128)S(1)}, f32[2,8,512]{2,1,0:T(8,128)S(1)}, u32[]{:S(2)}, u32[]{:S(2)}) collective-permute-start(f32[2,8,512]{2,1,0:T(8,128)S(1)} %add_add_fusion.3.here_ref), channel_id=1, source_target_pairs={{0,2},{2,0},{4,6},{6,4},{8,10},{10,8},{12,14},{14,12},{1,3},{3,1},... | collective-permute-start | bytes 98312 | tf_op jit(solution)/shard_map/ppermute | solution.py:444
  22.4 1.2 %collective-permute-start.4 = (f32[2,8,128]{2,1,0:T(8,128)S(1)}, f32[2,8,128]{2,1,0:T(8,128)S(1)}, u32[]{:S(2)}, u32[]{:S(2)}) collective-permute-start(f32[2,8,128]{2,1,0:T(8,128)S(1)} %get-tuple-element.47.own_ref), channel_id=1, source_target_pairs={{0,1},{1,0},{2,3},{3,2},{4,5},{5,4},{6,7},{7,6},{8,9},{9,8},{10,11... | collective-permute-start | bytes 24584 | tf_op jit(solution)/shard_map/ppermute | solution.py:433
  25.0 1.9 %collective-permute-start.6 = (f32[8,4096]{1,0:T(8,128)S(1)}, f32[8,4096]{1,0:T(8,128)S(1)}, u32[]{:S(2)}, u32[]{:S(2)}) collective-permute-start(f32[8,4096]{1,0:T(8,128)S(1)} %backward.8.refs_2_), channel_id=1, source_target_pairs={{0,1},{1,0},{2,3},{3,2},{4,5},{5,4},{6,7},{7,6},{8,9},{9,8},{10,11... | collective-permute-start | bytes 393224 | tf_op jit(solution)/shard_map/ppermute | solution.py:433
  26.5 1.5 %collective-permute-start.7 = (f32[8,4096]{1,0:T(8,128)S(1)}, f32[8,4096]{1,0:T(8,128)S(1)}, u32[]{:S(2)}, u32[]{:S(2)}) collective-permute-start(f32[8,4096]{1,0:T(8,128)S(1)} %backward.9.refs_2_), channel_id=1, source_target_pairs={{0,1},{1,0},{2,3},{3,2},{4,5},{5,4},{6,7},{7,6},{8,9},{9,8},{10,11... | collective-permute-start | bytes 393224 | tf_op jit(solution)/shard_map/ppermute | solution.py:433
  29.2 6.8 %collective-permute-start.10 = (f32[2,8,512]{2,1,0:T(8,128)S(1)}, f32[2,8,512]{2,1,0:T(8,128)S(1)}, u32[]{:S(2)}, u32[]{:S(2)}) collective-permute-start(f32[2,8,512]{2,1,0:T(8,128)S(1)} %get-tuple-element.56), channel_id=1, source_target_pairs={{0,12},{2,14},{4,8},{6,10},{8,4},{10,6},{12,0},{14,2},{1,13},{3,15... | collective-permute-start | bytes 98312 | tf_op jit(solution)/shard_map/ppermute | solution.py:444
  31.3 5.2 %collective-permute-start.9 = (f32[2,8,512]{2,1,0:T(8,128)S(1)}, f32[2,8,512]{2,1,0:T(8,128)S(1)}, u32[]{:S(2)}, u32[]{:S(2)}) collective-permute-start(f32[2,8,512]{2,1,0:T(8,128)S(1)} %get-tuple-element.56), channel_id=1, source_target_pairs={{0,8},{2,10},{4,12},{6,14},{8,0},{10,2},{12,4},{14,6},{1,9},{3,11}... | collective-permute-start | bytes 98312 | tf_op jit(solution)/shard_map/ppermute | solution.py:444
  31.3 5.1 %collective-permute-start.8 = (f32[2,8,512]{2,1,0:T(8,128)S(1)}, f32[2,8,512]{2,1,0:T(8,128)S(1)}, u32[]{:S(2)}, u32[]{:S(2)}) collective-permute-start(f32[2,8,512]{2,1,0:T(8,128)S(1)} %get-tuple-element.56), channel_id=1, source_target_pairs={{0,4},{2,6},{4,0},{6,2},{8,12},{10,14},{12,8},{14,10},{1,5},{3,7},... | collective-permute-start | bytes 98312 | tf_op jit(solution)/shard_map/ppermute | solution.py:444
  33.6 7.0 %collective-permute-start.13 = (f32[2,8,1024]{2,1,0:T(8,128)S(1)}, f32[2,8,1024]{2,1,0:T(8,128)S(1)}, u32[]{:S(2)}, u32[]{:S(2)}) collective-permute-start(f32[2,8,1024]{2,1,0:T(8,128)S(1)} %get-tuple-element.60), channel_id=1, source_target_pairs={{0,3},{2,5},{4,7},{6,9},{8,11},{10,13},{12,15},{3,0},{5,2},{7,4},{... | collective-permute-start | bytes 196616 | tf_op jit(solution)/shard_map/ppermute | solution.py:440
  36.4 4.0 %collective-permute-start.11 = (f32[2,8,512]{2,1,0:T(8,128)S(1)}, f32[2,8,512]{2,1,0:T(8,128)S(1)}, u32[]{:S(2)}, u32[]{:S(2)}) collective-permute-start(f32[2,8,512]{2,1,0:T(8,128)S(1)} %add_add_fusion.2.here_ref), channel_id=1, source_target_pairs={{0,2},{2,0},{4,6},{6,4},{8,10},{10,8},{12,14},{14,12},{1,3},{3,1},... | collective-permute-start | bytes 98312 | tf_op jit(solution)/shard_map/ppermute | solution.py:444
  40.5 1.2 %collective-permute-start.12 = (f32[2,8,128]{2,1,0:T(8,128)S(1)}, f32[2,8,128]{2,1,0:T(8,128)S(1)}, u32[]{:S(2)}, u32[]{:S(2)}) collective-permute-start(f32[2,8,128]{2,1,0:T(8,128)S(1)} %get-tuple-element.58.own_ref), channel_id=1, source_target_pairs={{0,1},{1,0},{2,3},{3,2},{4,5},{5,4},{6,7},{7,6},{8,9},{9,8},{10,11... | collective-permute-start | bytes 24584 | tf_op jit(solution)/shard_map/ppermute | solution.py:433
  43.1 1.9 %collective-permute-start.14 = (f32[8,4096]{1,0:T(8,128)S(1)}, f32[8,4096]{1,0:T(8,128)S(1)}, u32[]{:S(2)}, u32[]{:S(2)}) collective-permute-start(f32[8,4096]{1,0:T(8,128)S(1)} %backward.10.refs_2_), channel_id=1, source_target_pairs={{0,1},{1,0},{2,3},{3,2},{4,5},{5,4},{6,7},{7,6},{8,9},{9,8},{10,11... | collective-permute-start | bytes 393224 | tf_op jit(solution)/shard_map/ppermute | solution.py:433
  44.6 1.5 %collective-permute-start.15 = (f32[8,4096]{1,0:T(8,128)S(1)}, f32[8,4096]{1,0:T(8,128)S(1)}, u32[]{:S(2)}, u32[]{:S(2)}) collective-permute-start(f32[8,4096]{1,0:T(8,128)S(1)} %backward.11.refs_2_), channel_id=1, source_target_pairs={{0,1},{1,0},{2,3},{3,2},{4,5},{5,4},{6,7},{7,6},{8,9},{9,8},{10,11... | collective-permute-start | bytes 393224 | tf_op jit(solution)/shard_map/ppermute | solution.py:433
  47.4 6.8 %collective-permute-start.18 = (f32[2,8,512]{2,1,0:T(8,128)S(1)}, f32[2,8,512]{2,1,0:T(8,128)S(1)}, u32[]{:S(2)}, u32[]{:S(2)}) collective-permute-start(f32[2,8,512]{2,1,0:T(8,128)S(1)} %get-tuple-element.65), channel_id=1, source_target_pairs={{0,12},{2,14},{4,8},{6,10},{8,4},{10,6},{12,0},{14,2},{1,13},{3,15... | collective-permute-start | bytes 98312 | tf_op jit(solution)/shard_map/ppermute | solution.py:444
  49.6 4.8 %collective-permute-start.17 = (f32[2,8,512]{2,1,0:T(8,128)S(1)}, f32[2,8,512]{2,1,0:T(8,128)S(1)}, u32[]{:S(2)}, u32[]{:S(2)}) collective-permute-start(f32[2,8,512]{2,1,0:T(8,128)S(1)} %get-tuple-element.65), channel_id=1, source_target_pairs={{0,8},{2,10},{4,12},{6,14},{8,0},{10,2},{12,4},{14,6},{1,9},{3,11}... | collective-permute-start | bytes 98312 | tf_op jit(solution)/shard_map/ppermute | solution.py:444
  50.1 4.3 %collective-permute-start.16 = (f32[2,8,512]{2,1,0:T(8,128)S(1)}, f32[2,8,512]{2,1,0:T(8,128)S(1)}, u32[]{:S(2)}, u32[]{:S(2)}) collective-permute-start(f32[2,8,512]{2,1,0:T(8,128)S(1)} %get-tuple-element.65), channel_id=1, source_target_pairs={{0,4},{2,6},{4,0},{6,2},{8,12},{10,14},{12,8},{14,10},{1,5},{3,7},... | collective-permute-start | bytes 98312 | tf_op jit(solution)/shard_map/ppermute | solution.py:444
  51.8 6.8 %collective-permute-start.21 = (f32[2,8,1024]{2,1,0:T(8,128)S(1)}, f32[2,8,1024]{2,1,0:T(8,128)S(1)}, u32[]{:S(2)}, u32[]{:S(2)}) collective-permute-start(f32[2,8,1024]{2,1,0:T(8,128)S(1)} %get-tuple-element.69), channel_id=1, source_target_pairs={{0,3},{2,5},{4,7},{6,9},{8,11},{10,13},{12,15},{3,0},{5,2},{7,4},{... | collective-permute-start | bytes 196616 | tf_op jit(solution)/shard_map/ppermute | solution.py:440
  54.4 4.0 %collective-permute-start.19 = (f32[2,8,512]{2,1,0:T(8,128)S(1)}, f32[2,8,512]{2,1,0:T(8,128)S(1)}, u32[]{:S(2)}, u32[]{:S(2)}) collective-permute-start(f32[2,8,512]{2,1,0:T(8,128)S(1)} %add_add_fusion.1.here_ref), channel_id=1, source_target_pairs={{0,2},{2,0},{4,6},{6,4},{8,10},{10,8},{12,14},{14,12},{1,3},{3,1},... | collective-permute-start | bytes 98312 | tf_op jit(solution)/shard_map/ppermute | solution.py:444
  58.5 1.2 %collective-permute-start.20 = (f32[2,8,128]{2,1,0:T(8,128)S(1)}, f32[2,8,128]{2,1,0:T(8,128)S(1)}, u32[]{:S(2)}, u32[]{:S(2)}) collective-permute-start(f32[2,8,128]{2,1,0:T(8,128)S(1)} %get-tuple-element.67.own_ref), channel_id=1, source_target_pairs={{0,1},{1,0},{2,3},{3,2},{4,5},{5,4},{6,7},{7,6},{8,9},{9,8},{10,11... | collective-permute-start | bytes 24584 | tf_op jit(solution)/shard_map/ppermute | solution.py:433
  61.1 1.9 %collective-permute-start.22 = (f32[8,4096]{1,0:T(8,128)S(1)}, f32[8,4096]{1,0:T(8,128)S(1)}, u32[]{:S(2)}, u32[]{:S(2)}) collective-permute-start(f32[8,4096]{1,0:T(8,128)S(1)} %backward.12.refs_2_), channel_id=1, source_target_pairs={{0,1},{1,0},{2,3},{3,2},{4,5},{5,4},{6,7},{7,6},{8,9},{9,8},{10,11... | collective-permute-start | bytes 393224 | tf_op jit(solution)/shard_map/ppermute | solution.py:433
  62.6 1.5 %collective-permute-start.23 = (f32[8,4096]{1,0:T(8,128)S(1)}, f32[8,4096]{1,0:T(8,128)S(1)}, u32[]{:S(2)}, u32[]{:S(2)}) collective-permute-start(f32[8,4096]{1,0:T(8,128)S(1)} %backward.13.refs_2_), channel_id=1, source_target_pairs={{0,1},{1,0},{2,3},{3,2},{4,5},{5,4},{6,7},{7,6},{8,9},{9,8},{10,11... | collective-permute-start | bytes 393224 | tf_op jit(solution)/shard_map/ppermute | solution.py:433
  65.3 7.0 %collective-permute-start.26 = (f32[2,8,512]{2,1,0:T(8,128)S(1)}, f32[2,8,512]{2,1,0:T(8,128)S(1)}, u32[]{:S(2)}, u32[]{:S(2)}) collective-permute-start(f32[2,8,512]{2,1,0:T(8,128)S(1)} %get-tuple-element.74), channel_id=1, source_target_pairs={{0,12},{2,14},{4,8},{6,10},{8,4},{10,6},{12,0},{14,2},{1,13},{3,15... | collective-permute-start | bytes 98312 | tf_op jit(solution)/shard_map/ppermute | solution.py:444
  67.7 4.8 %collective-permute-start.25 = (f32[2,8,512]{2,1,0:T(8,128)S(1)}, f32[2,8,512]{2,1,0:T(8,128)S(1)}, u32[]{:S(2)}, u32[]{:S(2)}) collective-permute-start(f32[2,8,512]{2,1,0:T(8,128)S(1)} %get-tuple-element.74), channel_id=1, source_target_pairs={{0,8},{2,10},{4,12},{6,14},{8,0},{10,2},{12,4},{14,6},{1,9},{3,11}... | collective-permute-start | bytes 98312 | tf_op jit(solution)/shard_map/ppermute | solution.py:444
  68.3 4.3 %collective-permute-start.24 = (f32[2,8,512]{2,1,0:T(8,128)S(1)}, f32[2,8,512]{2,1,0:T(8,128)S(1)}, u32[]{:S(2)}, u32[]{:S(2)}) collective-permute-start(f32[2,8,512]{2,1,0:T(8,128)S(1)} %get-tuple-element.74), channel_id=1, source_target_pairs={{0,4},{2,6},{4,0},{6,2},{8,12},{10,14},{12,8},{14,10},{1,5},{3,7},... | collective-permute-start | bytes 98312 | tf_op jit(solution)/shard_map/ppermute | solution.py:444
  69.7 7.0 %collective-permute-start.29 = (f32[2,8,1024]{2,1,0:T(8,128)S(1)}, f32[2,8,1024]{2,1,0:T(8,128)S(1)}, u32[]{:S(2)}, u32[]{:S(2)}) collective-permute-start(f32[2,8,1024]{2,1,0:T(8,128)S(1)} %get-tuple-element.78), channel_id=1, source_target_pairs={{0,3},{2,5},{4,7},{6,9},{8,11},{10,13},{12,15},{3,0},{5,2},{7,4},{... | collective-permute-start | bytes 196616 | tf_op jit(solution)/shard_map/ppermute | solution.py:440
  72.6 4.0 %collective-permute-start.27 = (f32[2,8,512]{2,1,0:T(8,128)S(1)}, f32[2,8,512]{2,1,0:T(8,128)S(1)}, u32[]{:S(2)}, u32[]{:S(2)}) collective-permute-start(f32[2,8,512]{2,1,0:T(8,128)S(1)} %add_add_fusion.here_ref), channel_id=1, source_target_pairs={{0,2},{2,0},{4,6},{6,4},{8,10},{10,8},{12,14},{14,12},{1,3},{3,1},... | collective-permute-start | bytes 98312 | tf_op jit(solution)/shard_map/ppermute | solution.py:444
  76.7 1.2 %collective-permute-start.28 = (f32[2,8,128]{2,1,0:T(8,128)S(1)}, f32[2,8,128]{2,1,0:T(8,128)S(1)}, u32[]{:S(2)}, u32[]{:S(2)}) collective-permute-start(f32[2,8,128]{2,1,0:T(8,128)S(1)} %get-tuple-element.76.own_ref), channel_id=1, source_target_pairs={{0,1},{1,0},{2,3},{3,2},{4,5},{5,4},{6,7},{7,6},{8,9},{9,8},{10,11... | collective-permute-start | bytes 24584 | tf_op jit(solution)/shard_map/ppermute | solution.py:433
  79.2 1.9 %collective-permute-start.30 = (f32[8,4096]{1,0:T(8,128)S(1)}, f32[8,4096]{1,0:T(8,128)S(1)}, u32[]{:S(2)}, u32[]{:S(2)}) collective-permute-start(f32[8,4096]{1,0:T(8,128)S(1)} %backward.14.own_ref), channel_id=1, source_target_pairs={{0,1},{1,0},{2,3},{3,2},{4,5},{5,4},{6,7},{7,6},{8,9},{9,8},{10,11... | collective-permute-start | bytes 393224 | tf_op jit(solution)/shard_map/ppermute | solution.py:433
  80.7 1.4 %collective-permute-start.31 = (f32[8,4096]{1,0:T(8,128)S(1)}, f32[8,4096]{1,0:T(8,128)S(1)}, u32[]{:S(2)}, u32[]{:S(2)}) collective-permute-start(f32[8,4096]{1,0:T(8,128)S(1)} %backward.15.refs_3_), channel_id=1, source_target_pairs={{0,1},{1,0},{2,3},{3,2},{4,5},{5,4},{6,7},{7,6},{8,9},{9,8},{10,11... | collective-permute-start | bytes 393224 | tf_op jit(solution)/shard_map/ppermute | solution.py:433
  (4 other events, 89.1 us)
